TPU v7x, 256 devices: a whole 4x4x8 slice. The times are simulated.
256 devices in a mesh: inner: 64 (over y, x, z_hi), outer: 2 (over core), dp: 2 (over z_lo).
Axes of the slice: x: 4, y: 4, z: 8 (z_hi: 4, z_lo: 2; z = z_hi * 2 + z_lo), core: 2. Of those that a mesh axis runs over, the one named last changes fastest.
Arguments:
- inputs: bfloat16 [2, 256, 512, 768], P('dp', ('inner', 'outer')), may hold values from -6 to 6
- gate_in: bfloat16 [2, 256, 512, 768], P('dp', ('inner', 'outer')), may hold values from -6 to 6
- grad_out: bfloat16 [2, 256, 512, 768], P('dp', ('inner', 'outer')), may hold values from -6 to 6
- right_factor: bfloat16 [2, 512, 512], replicated, may hold values from -0.25 to 0.25
- left_factor: bfloat16 [2, 256, 256], replicated, may hold values from -0.375 to 0.375
Outputs:
- grad_inputs: bfloat16 [2, 256, 512, 768], P('dp', ('inner', 'outer'))
- grad_gate: bfloat16 [2, 256, 512, 768], P('dp', ('inner', 'outer'))
- grad_right: float32 [2, 512, 512], P('dp')
- grad_left: float32 [2, 256, 256], P('dp')
All inputs are finite; a program needn't handle non-finite values.
Results may differ from a plain program's by a relative error of at most 0.018.
Values may be sent and summed in bfloat16 or wider, within the bound.
A program may use at most 64 MiB of HBM per device.

v0:
```python
import jax
import jax.numpy as jnp
from jax import lax
from jax.sharding import PartitionSpec as P


def gelu_value(mixed):
    return mixed * (0.5 * (1.0 + jax.scipy.special.erf(mixed * 0.7071067811865476)))


def gelu_slope(mixed):
    normal_cdf = 0.5 * (1.0 + jax.scipy.special.erf(mixed * 0.7071067811865476))
    density = jnp.exp(-0.5 * mixed * mixed) * 0.3989422804014327
    return normal_cdf + mixed * density


def body(inputs, gate_in, grad_out, right_factor, left_factor):
    groups = right_factor.shape[0]
    local_rows = inputs.shape[1]
    cols = inputs.shape[2]
    chans = inputs.shape[3]
    width = chans // groups
    rows_all = left_factor.shape[1]
    count_inner = lax.axis_size("inner")
    count_outer = lax.axis_size("outer")
    col_share = cols // (count_inner * count_outer)
    x_wide = inputs[0].reshape(local_rows, cols, groups, width)
    mixed_cols = jnp.einsum(
        "gab,pbgc->pagc", right_factor, x_wide, preferred_element_type=jnp.float32
    ).astype(jnp.bfloat16)
    sending = (mixed_cols.reshape(1, local_rows, cols, chans), gate_in, grad_out)
    arrived = (
        lax.all_to_all(sending[0], ("inner", "outer"), split_axis=2, concat_axis=1, tiled=True),
        lax.all_to_all(sending[1], ("inner", "outer"), split_axis=2, concat_axis=1, tiled=True),
        lax.all_to_all(sending[2], ("inner", "outer"), split_axis=2, concat_axis=1, tiled=True),
    )
    cols_t = arrived[0].reshape(rows_all, col_share, groups, width)
    mixed = jnp.einsum("gpr,rqgc->pqgc", left_factor, cols_t, preferred_element_type=jnp.float32)
    mixed_b = mixed.astype(jnp.bfloat16)
    slope = gelu_slope(mixed)
    gate_t = arrived[1].reshape(rows_all, col_share, groups, width).astype(jnp.float32)
    grad_t = arrived[2].reshape(rows_all, col_share, groups, width).astype(jnp.float32)
    weighted = (grad_t * gate_t).astype(jnp.bfloat16)
    act = gelu_value(mixed_b.astype(jnp.float32))
    back_second = (grad_t * act).astype(jnp.bfloat16)
    grad_mixed = (weighted.astype(jnp.float32) * slope).astype(jnp.bfloat16)
    left_part = jnp.einsum("pqgc,rqgc->gpr", grad_mixed, cols_t, preferred_element_type=jnp.float32)
    grad_cols_t = jnp.einsum(
        "gpr,pqgc->rqgc", left_factor, grad_mixed, preferred_element_type=jnp.float32
    ).astype(jnp.bfloat16)
    returning = (
        grad_cols_t.reshape(1, rows_all, col_share, chans),
        back_second.reshape(1, rows_all, col_share, chans),
    )
    grad_cols, second = (
        lax.all_to_all(returning[0], ("inner", "outer"), split_axis=1, concat_axis=2, tiled=True),
        lax.all_to_all(returning[1], ("inner", "outer"), split_axis=1, concat_axis=2, tiled=True),
    )
    grad_cols = grad_cols.reshape(local_rows, cols, groups, width)
    right_part = jnp.einsum("pagc,pbgc->gab", grad_cols, x_wide, preferred_element_type=jnp.float32)
    grad_inputs = jnp.einsum(
        "gab,pagc->pbgc", right_factor, grad_cols, preferred_element_type=jnp.float32
    ).astype(jnp.bfloat16)
    summed = lax.psum((right_part, left_part), ("inner", "outer"))
    grad_right, grad_left = (
        lax.psum_scatter(summed[0], "dp", scatter_dimension=0, tiled=True),
        lax.psum_scatter(summed[1], "dp", scatter_dimension=0, tiled=True),
    )
    return (grad_inputs.reshape(1, local_rows, cols, chans), second, grad_right, grad_left)


def solution(mesh):
    placed = (
        P("dp", ("inner", "outer"), None, None),
        P("dp", ("inner", "outer"), None, None),
        P("dp", ("inner", "outer"), None, None),
        P(),
        P(),
    )
    return jax.shard_map(
        body,
        mesh=mesh,
        in_specs=placed,
        out_specs=(
            P("dp", ("inner", "outer"), None, None),
            P("dp", ("inner", "outer"), None, None),
            P("dp", None, None),
            P("dp", None, None),
        ),
        check_vma=False,
    )
```

profile of v0, /device:TPU:1, one launch (start us, length us, event | category | flops | bytes accessed | tf_op | source)
XLA Modules:
  0.0 1612.9 jit_solution(13625952069566669688)
XLA Ops:
  7.2 3.5 reshape_squeeze.3
  16.0 16.4 %all-to-all-start.2 = ((bf16[1,2,512,768]{3,1,0,2:T(2,128)(2,1)}), bf16[1,2,512,768]{3,1,0,2:T(2,128)(2,1)S(1)}, u32[]{:S(2)}, u32[]{:S(2)}) async-start(bf16[1,2,512,768]{3,1,0,2:T(2,128)(2,1)} %copy.66), calls=%async_computation.2 | async-start | bytes 3145728 | tf_op jit(solution)/shard_map/all_to_all | solution.py:33
  32.5 4.2 copy.60
  36.6 37.8 %all-to-all-done.2 = bf16[1,2,512,768]{3,1,0,2:T(2,128)(2,1)S(1)} async-done(((bf16[1,2,512,768]{3,1,0,2:T(2,128)(2,1)}), bf16[1,2,512,768]{3,1,0,2:T(2,128)(2,1)S(1)}, u32[]{:S(2)}, u32[]{:S(2)}) %all-to-all-start.2) | async-done | bytes 1572896 | tf_op jit(solution)/shard_map/all_to_all | solution.py:33
  74.4 8.7 all-to-all-start.1
  83.1 4.2 copy.58
  87.3 38.2 %all-to-all-done.1 = bf16[1,2,512,768]{3,1,0,2:T(2,128)(2,1)} async-done(((bf16[1,2,512,768]{3,1,0,2:T(2,128)(2,1)}), bf16[1,2,512,768]{3,1,0,2:T(2,128)(2,1)}, u32[]{:S(2)}, u32[]{:S(2)}) %all-to-all-start.1) | async-done | bytes 1572896 | tf_op jit(solution)/shard_map/all_to_all | solution.py:34
  125.5 7.2 all-to-all-start
  134.5 3.5 reshape.41
  138.0 3.7 copy.107
  141.7 5.4 reshape.47
  147.1 5.8 copy.63
  152.9 21.5 %all-to-all-done = bf16[1,2,512,768]{3,1,0,2:T(2,128)(2,1)} async-done(((bf16[1,2,512,768]{3,1,0,2:T(2,128)(2,1)}), bf16[1,2,512,768]{3,1,0,2:T(2,128)(2,1)}, u32[]{:S(2)}, u32[]{:S(2)}) %all-to-all-start) | async-done | bytes 1572896 | tf_op jit(solution)/shard_map/all_to_all | solution.py:35
  174.4 3.7 copy.108
  178.1 5.5 reshape.46
  183.6 5.9 copy.62
  189.6 5.7 fusion.13
  197.6 3.8 copy.70
  201.4 6.9 all-to-all-start.3
  211.6 40.8 %all-to-all-done.3 = bf16[1,256,4,768]{3,2,0,1:T(4,128)(2,1)} async-done(((bf16[1,256,4,768]{3,2,0,1:T(4,128)(2,1)}), bf16[1,256,4,768]{3,2,0,1:T(4,128)(2,1)}, u32[]{:S(2)}, u32[]{:S(2)}) %all-to-all-start.3) | async-done | bytes 1572896 | tf_op jit(solution)/shard_map/all_to_all | solution.py:56
  255.9 4.2 convolution_bitcast_fusion
  263.9 6.3 all-to-all-start.4
  270.3 54.4 %reduce-scatter.3.cloned.1.call-done = f32[1,512,512]{2,1,0:T(8,128)} async-done(((f32[2,512,512]{2,1,0:T(8,128)}), f32[1,512,512]{2,1,0:T(8,128)}) %reduce-scatter.3.cloned.1.call-update) | async-done | bytes 1048592 | tf_op jit(solution)/shard_map/reduce_scatter | solution.py:66
  334.1 1269.3 %all-reduce.3.cloned.1.call-done = (f32[1,512,512]{2,1,0:T(8,128)}, f32[1,256,256]{2,1,0:T(8,128)}) async-done(((f32[1,512,512]{2,1,0:T(8,128)}, f32[1,256,256]{2,1,0:T(8,128)}), (f32[1,512,512]{2,1,0:T(8,128)}, f32[1,256,256]{2,1,0:T(8,128)})) %all-reduce.3.cloned.1.call-update) | async-done | bytes 1310736 | tf_op jit(solution)/shard_map/psum | solution.py:64
  (38 shorter events, 32.3 us)
Async XLA Ops:
  7.2 4.7 copy-start
  10.7 1.1 copy-start.2
  16.0 58.3 %all-to-all-start.2 = ((bf16[1,2,512,768]{3,1,0,2:T(2,128)(2,1)}), bf16[1,2,512,768]{3,1,0,2:T(2,128)(2,1)S(1)}, u32[]{:S(2)}, u32[]{:S(2)}) async-start(bf16[1,2,512,768]{3,1,0,2:T(2,128)(2,1)} %copy.66), calls=%async_computation.2 | async-start | bytes 3145728 | tf_op jit(solution)/shard_map/all_to_all | solution.py:33
  74.4 51.1 %all-to-all-start.1 = ((bf16[1,2,512,768]{3,1,0,2:T(2,128)(2,1)}), bf16[1,2,512,768]{3,1,0,2:T(2,128)(2,1)}, u32[]{:S(2)}, u32[]{:S(2)}) async-start(bf16[1,2,512,768]{3,1,0,2:T(2,128)(2,1)} %copy.60), calls=%async_computation.1 | async-start | bytes 3145728 | tf_op jit(solution)/shard_map/all_to_all | solution.py:34
  125.5 48.9 %all-to-all-start = ((bf16[1,2,512,768]{3,1,0,2:T(2,128)(2,1)}), bf16[1,2,512,768]{3,1,0,2:T(2,128)(2,1)}, u32[]{:S(2)}, u32[]{:S(2)}) async-start(bf16[1,2,512,768]{3,1,0,2:T(2,128)(2,1)} %copy.58), calls=%async_computation | async-start | bytes 3145728 | tf_op jit(solution)/shard_map/all_to_all | solution.py:35
  183.6 5.9 copy-start.5
  195.2 1.2 copy-start.1
  201.4 51.0 %all-to-all-start.3 = ((bf16[1,256,4,768]{3,2,0,1:T(4,128)(2,1)}), bf16[1,256,4,768]{3,2,0,1:T(4,128)(2,1)}, u32[]{:S(2)}, u32[]{:S(2)}) async-start(bf16[1,256,4,768]{3,2,0,1:T(4,128)(2,1)} %copy.70), calls=%async_computation.3 | async-start | bytes 3145728 | tf_op jit(solution)/shard_map/all_to_all | solution.py:56
  208.3 61.9 %reduce-scatter.5.cloned.1.call-start = ((), (), s32[]{:S(2)}) async-start(), calls=%async_computation.8 | async-start | bytes 786432 | tf_op jit(solution)/shard_map/reduce_scatter | solution.py:67
  211.4 113.4 %reduce-scatter.3.cloned.1.call-start = ((), (), s32[]{:S(2)}) async-start(), calls=%async_computation.7 | async-start | bytes 3145728 | tf_op jit(solution)/shard_map/reduce_scatter | solution.py:66
  263.9 64.3 %all-to-all-start.4 = ((bf16[1,256,4,768]{3,2,0,1:T(4,128)(2,1)}), bf16[1,256,4,768]{3,2,0,1:T(4,128)(2,1)S(1)}, u32[]{:S(2)}, u32[]{:S(2)}) async-start(bf16[1,256,4,768]{3,2,0,1:T(4,128)(2,1)} %copy.76), calls=%async_computation.4 | async-start | bytes 3145728 | tf_op jit(solution)/shard_map/all_to_all | solution.py:57
  270.2 1333.1 %all-reduce.3.cloned.1.call-start = ((), (), s32[]{:S(2)}) async-start(), calls=%async_computation.9 | async-start | bytes 2621440 | tf_op jit(solution)/shard_map/psum | solution.py:64
  329.4 2.0 copy-start.3
  1603.3 2.3 copy-start.4
Sparse Core Ops, SparseCore 0:
  212.2 31.9 reduce-scatter.4
  260.3 64.4 reduce-scatter.2
  327.4 1275.8 all-reduce.2
where the time goes:
time: 1610 us
  waiting for transfers between devices  1470 us (91%)
  local copies, waits for them, and re-layouts  72 us (4%)
  starting transfers between devices  46 us (3%)
    psum x1, waiting for transfers between devices, body(): summed = lax.psum((right_part, left_part), ('inner', 'outer'))  1270 us
    reduce_scatter x1, waiting for transfers between devices, body(): lax.psum_scatter(summed[0], 'dp', scatter_dimension=0, tiled=True)  54.4 us
    all_to_all x1, waiting for transfers between devices, body(): lax.all_to_all(returning[0], ('inner', 'outer'), split_axis=1, concat_axi...  40.8 us
    all_to_all x1, waiting for transfers between devices, body(): lax.all_to_all(sending[1], ('inner', 'outer'), split_axis=2, concat_axis=...  38.2 us
    all_to_all x1, waiting for transfers between devices, body(): lax.all_to_all(sending[0], ('inner', 'outer'), split_axis=2, concat_axis=...  37.8 us
  transfers between devices with their start and end apart: 8, of which 7 were waited for; matrix products, arithmetic and copies ran while one was open for 3% of the time, Pallas kernels for 0%

commit v1 on v0

v1 whole, which is shorter than its diff:
```python
import jax
import jax.numpy as jnp
from jax import lax
from jax.experimental import pallas as pl
from jax.experimental.pallas import tpu as pltpu
from jax.sharding import PartitionSpec as P

MESH = pl.DeviceIdType.MESH
F32 = jnp.float32
BF16 = jnp.bfloat16

INNER = 64
ZH = 4
XY = 16
PEERS = 128
ROWS = 2
CG = 384
LANES = CG // 128
Q = 512
P_ALL = 256
QB = 8
BLK = ROWS * QB
FIRST, SECOND, THIRD = 1, 2, 3


def gelu_value(mixed):
    return mixed * (0.5 * (1.0 + lax.erf(mixed * 0.7071067811865476)))


def gelu_slope(mixed):
    normal_cdf = 0.5 * (1.0 + lax.erf(mixed * 0.7071067811865476))
    density = jnp.exp(-0.5 * mixed * mixed) * 0.3989422804014327
    return normal_cdf + mixed * density


def wait_bytes(ref, sem):
    pltpu.make_async_copy(ref, ref, sem).wait()


def dot(a, b, ca, cb):
    return lax.dot_general(a, b, (((ca,), (cb,)), ((), ())), preferred_element_type=F32)


def kernel(
    x, gate, gout, rf, lf,
    gin_o, ggate_o, gr_o, gl_o,
    s1, s2, r1, r2, t1, t2, b1, b2,
    wide_a, wide_b, slope, colsb, gcb, rt, lt,
    grp, cx, rs_s, rs_r, ls_s, ls_r, share, zrecv, fin,
    a_send, a_recv, m_send, m_recv, q_send, q_recv,
):
    i = lax.axis_index("inner")
    c = lax.axis_index("outer")
    d = lax.axis_index("dp")
    me = i * 2 + c
    zh = i % ZH
    j = i // ZH
    yy = j // 4
    xx = j % 4

    barrier = pltpu.get_barrier_semaphore()

    def greet(k, _):
        s = (me + k) % PEERS
        pl.semaphore_signal(barrier, inc=1, device_id={"inner": s // 2, "outer": s % 2}, device_id_type=MESH)
        return 0

    lax.fori_loop(1, PEERS, greet, 0)

    def greet_z(k, _):
        pl.semaphore_signal(
            barrier, inc=1, device_id={"inner": j * ZH + (zh + k) % ZH, "dp": 1 - d}, device_id_type=MESH
        )
        return 0

    lax.fori_loop(0, ZH, greet_z, 0)

    def right_mix(m, _):
        for g in range(2):
            lhs = rf[g, pl.ds(pl.multiple_of(m * 128, 128), 128), :]
            parts = [
                dot(lhs, x[0, p, :, g * CG:(g + 1) * CG], 1, 0).reshape(16, QB, CG) for p in range(ROWS)
            ]
            s1[g, pl.ds(m * 16, 16)] = jnp.concatenate(parts, axis=1).astype(BF16)
        return 0

    lax.fori_loop(0, 4, right_mix, 0)

    pl.semaphore_wait(barrier, PEERS - 1 + ZH)

    def partner(k, dy):
        jj = ((yy + dy) % 4) * 4 + (xx + k // 8) % 4
        return jj * ZH + (zh + (k // 2) % 4) % ZH, (c + k) % 2

    def send_out(src, dst, n):
        for dy in range(4):
            def step(k, _):
                ii, cc = partner(k, dy)
                pltpu.make_async_remote_copy(
                    src_ref=src.at[cc, ii], dst_ref=dst.at[me], send_sem=a_send.at[n], recv_sem=a_recv.at[n],
                    device_id={"inner": ii, "outer": cc}, device_id_type=MESH,
                ).start()
                return 0

            lax.fori_loop(1 if dy == 0 else 0, 32, step, 0)

    def send_back(src, dst, n, dy):
        def step(k, _):
            ii, cc = partner(k, dy)
            pltpu.make_async_remote_copy(
                src_ref=src.at[ii * 2 + cc], dst_ref=dst.at[c, j, zh], send_sem=a_send.at[n],
                recv_sem=a_recv.at[4 * n - 6 + dy],
                device_id={"inner": ii, "outer": cc}, device_id_type=MESH,
            ).start()
            return 0

        lax.fori_loop(1 if dy == 0 else 0, 32, step, 0)

    def wait_back(n, dy):
        wait_bytes(t1.at[pl.ds(0, 31 if dy == 0 else 32)], a_recv.at[4 * n - 6 + dy])

    send_out(s1, r1, 0)

    def weigh(m, _):
        rows = pl.ds(pl.multiple_of(m * 64, 64), 64)
        for g in range(2):
            parts = []
            for p in range(ROWS):
                a = gout[0, p, rows, g * CG:(g + 1) * CG].astype(F32)
                b = gate[0, p, rows, g * CG:(g + 1) * CG].astype(F32)
                parts.append((a * b).reshape(8, QB, CG))
            s2[g, pl.ds(m * 8, 8)] = jnp.concatenate(parts, axis=1).astype(BF16)
        return 0

    lax.fori_loop(0, 8, weigh, 0)
    send_out(s2, r2, 1)

    r1[me] = s1[c, i]
    r2[me] = s2[c, i]
    lfac = lf[c]
    lt[...] = lfac.astype(F32).T.astype(BF16)
    for g in range(2):
        for h in range(2):
            rt[g, :, h * 256:(h + 1) * 256] = rf[g, h * 256:(h + 1) * 256, :].astype(F32).T.astype(BF16)

    def widen(src):
        def step(m, _):
            v = src[pl.ds(m * 4, 4)].reshape(64, CG).astype(F32)
            for n in range(LANES):
                wide_a[n, pl.ds(pl.multiple_of(m * 64, 64), 64), :] = v[:, n * 128:(n + 1) * 128]
            return 0

        lax.fori_loop(0, 32, step, 0)

    def narrow(dst):
        def step(m, _):
            for n in range(LANES):
                v = wide_b[n, pl.ds(pl.multiple_of(m * 64, 64), 64), :].astype(BF16)
                dst[pl.ds(m * 4, 4), :, n * 128:(n + 1) * 128] = v.reshape(4, BLK, 128)
            return 0

        lax.fori_loop(0, 32, step, 0)

    def column(q):
        return jnp.concatenate([wide_a[n, pl.ds(q, P_ALL, stride=QB), :] for n in range(LANES)], axis=1)

    def put_column(q, v):
        for n in range(LANES):
            wide_b[n, pl.ds(q, P_ALL, stride=QB), :] = v[:, n * 128:(n + 1) * 128]

    wait_bytes(r1.at[pl.ds(0, PEERS - 1)], a_recv.at[0])
    widen(r1)
    for q in range(QB):
        xq = column(q).astype(BF16)
        colsb[q] = xq
        mixed = dot(lfac, xq, 1, 0)
        put_column(q, mixed)
        slope[q] = mixed
    narrow(t1)
    b1[c, j, zh] = t1[me]
    for dy in range(FIRST):
        send_back(t1, b1, 2, dy)

    def slopes(m, _):
        rows = pl.ds(pl.multiple_of((m % 4) * 64, 64), 64)
        slope[m // 4, rows, :] = gelu_slope(slope[m // 4, rows, :])
        return 0

    lax.fori_loop(0, QB * 4, slopes, 0)

    wait_bytes(r2.at[pl.ds(0, PEERS - 1)], a_recv.at[1])
    widen(r2)
    gl_acc = jnp.zeros((P_ALL, P_ALL), F32)
    for q in range(QB):
        gm = (column(q) * slope[q]).astype(BF16)
        put_column(q, dot(lt[...], gm, 1, 0))
        gl_acc = gl_acc + dot(gm, colsb[q], 1, 1)
    narrow(t2)
    b2[c, j, zh] = t2[me]
    for dy in range(4):
        send_back(t2, b2, 3, dy)
    for dy in range(FIRST, SECOND):
        send_back(t1, b1, 2, dy)
    ls_s[...] = gl_acc.astype(BF16).reshape(XY, 16, P_ALL)

    def scatter(src, dst, n, dy):
        y2 = (yy + 4 - dy) % 4

        def step(k, _):
            jj = y2 * 4 + (xx + k) % 4
            pltpu.make_async_remote_copy(
                src_ref=src.at[jj], dst_ref=dst.at[j], send_sem=m_send.at[n], recv_sem=m_recv.at[n],
                device_id={"inner": jj * ZH + zh}, device_id_type=MESH,
            ).start()
            return 0

        lax.fori_loop(1 if dy == 0 else 0, 4, step, 0)

    for dy in range(4):
        scatter(ls_s, ls_r, 0, dy)
    ls_r[j] = ls_s[j]

    def gate_grad(dy):
        wait_back(2, dy)
        y2 = (yy + 4 - dy) % 4

        def step(m, _):
            for g in range(2):
                cols = slice(g * CG, (g + 1) * CG)
                v = b1[g, pl.ds(y2 * 4 + m * 2, 2)].reshape(8, BLK, CG).astype(F32)
                rows = pl.ds(pl.multiple_of(y2 * 128 + m * 64, 64), 64)
                for p in range(ROWS):
                    act = gelu_value(v[:, p * QB:(p + 1) * QB, :].reshape(64, CG))
                    ggate_o[0, p, rows, cols] = (gout[0, p, rows, cols].astype(F32) * act).astype(BF16)
            return 0

        lax.fori_loop(0, 2, step, 0)

    for dy in range(FIRST):
        gate_grad(dy)

    def swap(dy):
        rows = pl.ds(pl.multiple_of(((yy + 4 - dy) % 4) * 128, 128), 128)
        return pltpu.make_async_remote_copy(
            src_ref=grp.at[1 - c, rows], dst_ref=cx.at[rows], send_sem=q_send.at[dy], recv_sem=q_recv.at[dy],
            device_id={"outer": 1 - c}, device_id_type=MESH,
        )

    def finish(dy):
        swap(dy).wait()
        y2 = (yy + 4 - dy) % 4

        def step(m, _):
            rows = pl.ds(pl.multiple_of(y2 * 128 + m * 32, 32), 32)
            rs_s[y2 * 4 + m] = (grp[c, rows, :] + cx[rows, :]).astype(BF16)
            return 0

        lax.fori_loop(0, 4, step, 0)
        scatter(rs_s, rs_r, 2, dy)

    for dy in range(4):
        wait_back(3, dy)
        y2 = (yy + 4 - dy) % 4
        rows = pl.ds(pl.multiple_of(y2 * 128, 128), 128)
        for g in range(2):
            cols = slice(g * CG, (g + 1) * CG)
            v = b2[g, pl.ds(y2 * 4, 4)].reshape(16, BLK, CG).astype(F32)
            total = None
            for p in range(ROWS):
                part = v[:, p * QB:(p + 1) * QB, :].reshape(128, CG).astype(BF16)
                gcb[p, rows, cols] = part
                term = dot(part, x[0, p, :, cols], 1, 1)
                total = term if total is None else total + term
            grp[g, rows, :] = total
        swap(dy).start()
        if dy > 0:
            finish(dy - 1)
    finish(3)
    rs_r[j] = rs_s[j]
    for dy in range(SECOND, THIRD):
        send_back(t1, b1, 2, dy)

    def input_grad(m, _):
        rows = pl.ds(pl.multiple_of(m * 128, 128), 128)
        for g in range(2):
            cols = slice(g * CG, (g + 1) * CG)
            for p in range(ROWS):
                gin_o[0, p, rows, cols] = dot(rt[g, rows, :], gcb[p, :, cols], 1, 0).astype(BF16)
        return 0

    lax.fori_loop(0, 4, input_grad, 0)

    wait_bytes(ls_r.at[pl.ds(0, XY - 1)], m_recv.at[0])
    wait_bytes(rs_r.at[pl.ds(0, XY - 1)], m_recv.at[2])
    gr_sum = rs_r[0].astype(F32)
    gl_sum = ls_r[0].astype(F32)
    for k in range(1, XY):
        gr_sum = gr_sum + rs_r[k].astype(F32)
        gl_sum = gl_sum + ls_r[k].astype(F32)
    share[0:32, :] = gr_sum[:, 0:256].astype(BF16)
    share[32:64, :] = gr_sum[:, 256:512].astype(BF16)
    share[64:80, :] = gl_sum.astype(BF16)

    def to_z(k):
        return pltpu.make_async_remote_copy(
            src_ref=share, dst_ref=zrecv.at[zh * 2 + d], send_sem=m_send.at[3], recv_sem=m_recv.at[3],
            device_id={"inner": j * ZH + (zh + k) % ZH, "dp": c}, device_id_type=MESH,
        )

    for k in range(1, ZH):
        to_z(k).start()

    @pl.when(d != c)
    def _():
        to_z(0).start()

    for dy in range(THIRD, 4):
        send_back(t1, b1, 2, dy)
    for dy in range(FIRST, SECOND):
        gate_grad(dy)

    @pl.when(d == c)
    def _():
        zrecv[zh * 2 + d] = share[...]
        wait_bytes(zrecv.at[pl.ds(0, 7)], m_recv.at[3])
        total = zrecv[0].astype(F32)
        for k in range(1, 8):
            total = total + zrecv[k].astype(F32)
        fin[j] = total.astype(BF16)

        def give(k, _):
            jj = (j + k) % XY
            pltpu.make_async_remote_copy(
                src_ref=fin.at[j], dst_ref=fin.at[j], send_sem=m_send.at[4], recv_sem=m_recv.at[4],
                device_id={"inner": jj * ZH + zh}, device_id_type=MESH,
            ).start()
            return 0

        lax.fori_loop(1, XY, give, 0)

    for dy in range(SECOND, 4):
        gate_grad(dy)

    @pl.when(d == c)
    def _():
        wait_bytes(fin.at[pl.ds(0, XY - 1)], m_recv.at[4])
        over = pltpu.make_async_remote_copy(
            src_ref=fin, dst_ref=fin, send_sem=m_send.at[5], recv_sem=m_recv.at[5],
            device_id={"outer": 1 - c}, device_id_type=MESH,
        )
        over.start()
        wait_bytes(fin.at[pl.ds(0, XY - 1)], m_send.at[4])
        wait_bytes(zrecv.at[pl.ds(0, 3)], m_send.at[3])
        wait_bytes(fin, m_send.at[5])

    @pl.when(d != c)
    def _():
        wait_bytes(zrecv.at[pl.ds(0, 4)], m_send.at[3])
        wait_bytes(fin, m_recv.at[5])

    for k in range(XY):
        gr_o[0, k * 32:(k + 1) * 32, 0:256] = fin[k, 0:32, :].astype(F32)
        gr_o[0, k * 32:(k + 1) * 32, 256:512] = fin[k, 32:64, :].astype(F32)
        gl_o[0, k * 16:(k + 1) * 16, :] = fin[k, 64:80, :].astype(F32)

    for n in range(4):
        wait_bytes(r1.at[pl.ds(0, PEERS - 1)], a_send.at[n])
    wait_bytes(ls_r.at[pl.ds(0, XY - 1)], m_send.at[0])
    wait_bytes(rs_r.at[pl.ds(0, XY - 1)], m_send.at[2])


def body(inputs, gate_in, grad_out, right_factor, left_factor):
    vmem = pl.BlockSpec(memory_space=pltpu.VMEM)
    out_shape = (
        jax.ShapeDtypeStruct((1, ROWS, Q, 2 * CG), BF16),
        jax.ShapeDtypeStruct((1, ROWS, Q, 2 * CG), BF16),
        jax.ShapeDtypeStruct((1, Q, Q), F32),
        jax.ShapeDtypeStruct((1, P_ALL, P_ALL), F32),
    )
    scratch = [
        pltpu.VMEM((2, INNER, BLK, CG), BF16),
        pltpu.VMEM((2, INNER, BLK, CG), BF16),
        pltpu.VMEM((PEERS, BLK, CG), BF16),
        pltpu.VMEM((PEERS, BLK, CG), BF16),
        pltpu.VMEM((PEERS, BLK, CG), BF16),
        pltpu.VMEM((PEERS, BLK, CG), BF16),
        pltpu.VMEM((2, XY, ZH, BLK, CG), BF16),
        pltpu.VMEM((2, XY, ZH, BLK, CG), BF16),
        pltpu.VMEM((LANES, PEERS * BLK, 128), F32),
        pltpu.VMEM((LANES, PEERS * BLK, 128), F32),
        pltpu.VMEM((QB, P_ALL, CG), F32),
        pltpu.VMEM((QB, P_ALL, CG), BF16),
        pltpu.VMEM((ROWS, Q, 2 * CG), BF16),
        pltpu.VMEM((2, Q, Q), BF16),
        pltpu.VMEM((P_ALL, P_ALL), BF16),
        pltpu.VMEM((2, Q, Q), F32),
        pltpu.VMEM((Q, Q), F32),
        pltpu.VMEM((XY, 32, Q), BF16),
        pltpu.VMEM((XY, 32, Q), BF16),
        pltpu.VMEM((XY, 16, P_ALL), BF16),
        pltpu.VMEM((XY, 16, P_ALL), BF16),
        pltpu.VMEM((80, 256), BF16),
        pltpu.VMEM((8, 80, 256), BF16),
        pltpu.VMEM((XY, 80, 256), BF16),
        pltpu.SemaphoreType.DMA((4,)),
        pltpu.SemaphoreType.DMA((10,)),
        pltpu.SemaphoreType.DMA((6,)),
        pltpu.SemaphoreType.DMA((6,)),
        pltpu.SemaphoreType.DMA((4,)),
        pltpu.SemaphoreType.DMA((4,)),
    ]
    return pl.pallas_call(
        kernel,
        out_shape=out_shape,
        in_specs=[vmem] * 5,
        out_specs=(vmem,) * 4,
        scratch_shapes=scratch,
        compiler_params=pltpu.CompilerParams(
            collective_id=0, has_side_effects=True, vmem_limit_bytes=56 * 1024 * 1024
        ),
        cost_estimate=pl.CostEstimate(flops=4 * 10**9, bytes_accessed=12 * 10**6, transcendentals=3 * 10**6),
    )(inputs, gate_in, grad_out, right_factor, left_factor)


def solution(mesh):
    rows = P("dp", ("inner", "outer"), None, None)
    return jax.shard_map(
        body,
        mesh=mesh,
        in_specs=(rows, rows, rows, P(), P()),
        out_specs=(rows, rows, P("dp", None, None), P("dp", None, None)),
        check_vma=False,
    )
```

time: 1610 us -> 184 us (0.11)
  waiting for transfers between devices: 1470 us -> 0 us
  Pallas kernels: 0 us -> 177 us
  local copies, waits for them, and re-layouts: 72 us -> 6.36 us
  starting transfers between devices: 46 us -> 0 us
    psum x1 -> x0, waiting for transfers between devices: 1270 us -> none  [body(): summed = lax.psum((right_part, left_part), ('inner', 'outer'))]
    pallas_call x0 -> x1, Pallas kernels: none -> 177 us  [body(): pl.pallas_call(kernel, out_shape=out_shape, in_specs=[vmem] * 5, out_spec...]
    all_to_all x5 -> x0, waiting for transfers between devices: 142 us -> none  [the longest x1 40.8 us: body(): lax.all_to_all(returning[0], ('inner', 'outer'), split_axis=1, concat_axi...]
    reduce_scatter x2 -> x0, waiting for transfers between devices: 54.5 us -> none  [the longest x1 54.4 us: body(): lax.psum_scatter(summed[0], 'dp', scatter_dimension=0, tiled=True)]
    all_to_all x5 -> x0, starting transfers between devices: 45.6 us -> none  [the longest x1 16.4 us: body(): lax.all_to_all(sending[0], ('inner', 'outer'), split_axis=2, concat_axis=...]
    convert_element_type x10 -> x0, local copies, waits for them, and re-layouts: 33 us -> none  [the longest x3 15.1 us: body(): arrived[2].reshape(rows_all, col_share, groups, width).astype(jnp.float32)]
  transfers between devices with their start and end apart: 8 -> 0, of which waited for: 7 -> 0; matrix products, arithmetic and copies ran while one was open for 3% -> 0% of each run, Pallas kernels for 0% -> 0%
where the time goes in v1:
time: 184 us
  Pallas kernels  177 us (96%)
  local copies, waits for them, and re-layouts  6.36 us (3%)
    pallas_call x1, Pallas kernels, body(): pl.pallas_call(kernel, out_shape=out_shape, in_specs=[vmem] * 5, out_spec...  177 us
    unnamed x10, local copies, waits for them, and re-layouts  6.36 us

profile of v1, /device:TPU:1, one launch (start us, length us, event | category | flops | bytes accessed | tf_op | source)
XLA Modules:
  0.0 184.3 jit_solution(10347889445999068140)
XLA Ops:
  0.6 177.3 %shard_map.84 = (bf16[1,2,512,768]{3,2,1,0:T(8,128)(2,1)}, bf16[1,2,512,768]{3,2,1,0:T(8,128)(2,1)}, f32[1,512,512]{2,1,0:T(8,128)}, f32[1,256,256]{2,1,0:T(8,128)}) custom-call(bf16[1,2,512,768]{3,2,1,0:T(8,128)(2,1)} %x.1, bf16[1,2,512,768]{3,2,1,0:T(8,128)(2,1)} %gate.1, bf16[1,2,512,768]{3,2,1,0:T(8,128)(2,1)} %gout.1, bf16[2,512,512]{2,1,0:T(8,128)(2,1)} %rf.1, ...), custom_call_target="tpu_custom_call" | custom-call | flops 4000000000 | bytes 12000000 | tf_op jit(solution)/shard_map/pallas_call | solution.py:412
  177.9 0.0 copy-start
  177.9 2.8 %copy.13 = bf16[1,2,512,768]{3,2,1,0:T(8,128)(2,1)} copy(bf16[1,2,512,768]{3,2,1,0:T(8,128)(2,1)} %get-tuple-element.8) | data formatting | bytes 3145728
  180.7 0.0 copy-done
  180.7 0.0 copy-start.1
  180.7 1.1 copy.14
  181.9 0.6 copy-done.1
  182.5 0.0 copy-start.2
  182.5 1.0 copy.15
  183.5 0.1 copy-done.2
  183.6 0.7 copy.16
Async XLA Ops:
  177.9 2.8 %copy-start = (bf16[1,2,512,768]{3,2,1,0:T(8,128)(2,1)S(1)}, bf16[1,2,512,768]{3,2,1,0:T(8,128)(2,1)}, u32[]{:S(2)}) copy-start(bf16[1,2,512,768]{3,2,1,0:T(8,128)(2,1)} %get-tuple-element.9) | copy-start | bytes 4718596
  180.7 1.8 copy-start.1
  182.5 1.1 copy-start.2

commit v2 on v1

--- a/solution.py
+++ b/solution.py
@@ -42,12 +42,13 @@
 
 
 def kernel(
-    x, gate, gout, rf, lf,
+    x_h, gate_h, gout_h, rf_h, lf_h,
     gin_o, ggate_o, gr_o, gl_o,
     s1, s2, r1, r2, t1, t2, b1, b2,
-    wide_a, wide_b, slope, colsb, gcb, rt, lt,
+    x, gate, gout, rf, lf, gin_v, ggate_v, gr_v, gl_v,
+    wide_a, wide_b, slope, colsb, gmb, gcb, rt, lt,
     grp, cx, rs_s, rs_r, ls_s, ls_r, share, zrecv, fin,
-    a_send, a_recv, m_send, m_recv, q_send, q_recv,
+    a_send, a_recv, m_send, m_recv, q_send, q_recv, l_sem,
 ):
     i = lax.axis_index("inner")
     c = lax.axis_index("outer")
@@ -58,6 +59,15 @@
     yy = j // 4
     xx = j % 4
 
+    loads = [
+        pltpu.make_async_copy(src, dst, l_sem.at[n])
+        for n, (src, dst) in enumerate(
+            ((x_h.at[0], x), (rf_h, rf), (gate_h.at[0], gate), (gout_h.at[0], gout), (lf_h, lf))
+        )
+    ]
+    for load in loads:
+        load.start()
+
     barrier = pltpu.get_barrier_semaphore()
 
     def greet(k, _):
@@ -75,11 +85,14 @@
 
     lax.fori_loop(0, ZH, greet_z, 0)
 
+    loads[0].wait()
+    loads[1].wait()
+
     def right_mix(m, _):
         for g in range(2):
             lhs = rf[g, pl.ds(pl.multiple_of(m * 128, 128), 128), :]
             parts = [
-                dot(lhs, x[0, p, :, g * CG:(g + 1) * CG], 1, 0).reshape(16, QB, CG) for p in range(ROWS)
+                dot(lhs, x[p, :, g * CG:(g + 1) * CG], 1, 0).reshape(16, QB, CG) for p in range(ROWS)
             ]
             s1[g, pl.ds(m * 16, 16)] = jnp.concatenate(parts, axis=1).astype(BF16)
         return 0
@@ -88,46 +101,52 @@
 
     pl.semaphore_wait(barrier, PEERS - 1 + ZH)
 
-    def partner(k, dy):
-        jj = ((yy + dy) % 4) * 4 + (xx + k // 8) % 4
-        return jj * ZH + (zh + (k // 2) % 4) % ZH, (c + k) % 2
+    def place(e, t, sign):
+        return ((yy + sign * (e + t) + 8) % 4) * 4 + (xx + sign * t + 4) % 4
+
+    def partner(k, e):
+        jj = place(e, k % 4, 1)
+        return jj * ZH + (zh + k % 4 + k // 4) % ZH, (c + k // 16) % 2
 
     def send_out(src, dst, n):
-        for dy in range(4):
+        for e in range(4):
             def step(k, _):
-                ii, cc = partner(k, dy)
+                ii, cc = partner(k, e)
                 pltpu.make_async_remote_copy(
                     src_ref=src.at[cc, ii], dst_ref=dst.at[me], send_sem=a_send.at[n], recv_sem=a_recv.at[n],
                     device_id={"inner": ii, "outer": cc}, device_id_type=MESH,
                 ).start()
                 return 0
 
-            lax.fori_loop(1 if dy == 0 else 0, 32, step, 0)
-
-    def send_back(src, dst, n, dy):
+            lax.fori_loop(1 if e == 0 else 0, 32, step, 0)
+
+    def send_back(src, dst, n, e):
         def step(k, _):
-            ii, cc = partner(k, dy)
+            ii, cc = partner(k, e)
             pltpu.make_async_remote_copy(
                 src_ref=src.at[ii * 2 + cc], dst_ref=dst.at[c, j, zh], send_sem=a_send.at[n],
-                recv_sem=a_recv.at[4 * n - 6 + dy],
+                recv_sem=a_recv.at[4 * n - 6 + e],
                 device_id={"inner": ii, "outer": cc}, device_id_type=MESH,
             ).start()
             return 0
 
-        lax.fori_loop(1 if dy == 0 else 0, 32, step, 0)
-
-    def wait_back(n, dy):
-        wait_bytes(t1.at[pl.ds(0, 31 if dy == 0 else 32)], a_recv.at[4 * n - 6 + dy])
+        lax.fori_loop(1 if e == 0 else 0, 32, step, 0)
+
+    def wait_back(n, e):
+        wait_bytes(t1.at[pl.ds(0, 31 if e == 0 else 32)], a_recv.at[4 * n - 6 + e])
 
     send_out(s1, r1, 0)
+
+    loads[2].wait()
+    loads[3].wait()
 
     def weigh(m, _):
         rows = pl.ds(pl.multiple_of(m * 64, 64), 64)
         for g in range(2):
             parts = []
             for p in range(ROWS):
-                a = gout[0, p, rows, g * CG:(g + 1) * CG].astype(F32)
-                b = gate[0, p, rows, g * CG:(g + 1) * CG].astype(F32)
+                a = gout[p, rows, g * CG:(g + 1) * CG].astype(F32)
+                b = gate[p, rows, g * CG:(g + 1) * CG].astype(F32)
                 parts.append((a * b).reshape(8, QB, CG))
             s2[g, pl.ds(m * 8, 8)] = jnp.concatenate(parts, axis=1).astype(BF16)
         return 0
@@ -137,6 +156,7 @@
 
     r1[me] = s1[c, i]
     r2[me] = s2[c, i]
+    loads[4].wait()
     lfac = lf[c]
     lt[...] = lfac.astype(F32).T.astype(BF16)
     for g in range(2):
@@ -178,8 +198,8 @@
         slope[q] = mixed
     narrow(t1)
     b1[c, j, zh] = t1[me]
-    for dy in range(FIRST):
-        send_back(t1, b1, 2, dy)
+    for e in range(FIRST):
+        send_back(t1, b1, 2, e)
 
     def slopes(m, _):
         rows = pl.ds(pl.multiple_of((m % 4) * 64, 64), 64)
@@ -190,105 +210,107 @@
 
     wait_bytes(r2.at[pl.ds(0, PEERS - 1)], a_recv.at[1])
     widen(r2)
-    gl_acc = jnp.zeros((P_ALL, P_ALL), F32)
     for q in range(QB):
         gm = (column(q) * slope[q]).astype(BF16)
         put_column(q, dot(lt[...], gm, 1, 0))
-        gl_acc = gl_acc + dot(gm, colsb[q], 1, 1)
+        gmb[q] = gm
     narrow(t2)
     b2[c, j, zh] = t2[me]
-    for dy in range(4):
-        send_back(t2, b2, 3, dy)
-    for dy in range(FIRST, SECOND):
-        send_back(t1, b1, 2, dy)
+    for e in range(4):
+        send_back(t2, b2, 3, e)
+    for e in range(FIRST, SECOND):
+        send_back(t1, b1, 2, e)
+    gl_acc = jnp.zeros((P_ALL, P_ALL), F32)
+    for q in range(QB):
+        gl_acc = gl_acc + dot(gmb[q], colsb[q], 1, 1)
     ls_s[...] = gl_acc.astype(BF16).reshape(XY, 16, P_ALL)
 
-    def scatter(src, dst, n, dy):
-        y2 = (yy + 4 - dy) % 4
-
-        def step(k, _):
-            jj = y2 * 4 + (xx + k) % 4
+    def scatter(src, dst, n, e):
+        def step(t, _):
+            jj = place(e, t, -1)
             pltpu.make_async_remote_copy(
                 src_ref=src.at[jj], dst_ref=dst.at[j], send_sem=m_send.at[n], recv_sem=m_recv.at[n],
                 device_id={"inner": jj * ZH + zh}, device_id_type=MESH,
             ).start()
             return 0
 
-        lax.fori_loop(1 if dy == 0 else 0, 4, step, 0)
-
-    for dy in range(4):
-        scatter(ls_s, ls_r, 0, dy)
+        lax.fori_loop(1 if e == 0 else 0, 4, step, 0)
+
+    for e in range(4):
+        scatter(ls_s, ls_r, 0, e)
     ls_r[j] = ls_s[j]
 
-    def gate_grad(dy):
-        wait_back(2, dy)
-        y2 = (yy + 4 - dy) % 4
-
-        def step(m, _):
+    def gate_grad(e):
+        wait_back(2, e)
+
+        def step(t, _):
+            jj = place(e, t, -1)
+            rows = pl.ds(pl.multiple_of(jj * 32, 32), 32)
             for g in range(2):
                 cols = slice(g * CG, (g + 1) * CG)
-                v = b1[g, pl.ds(y2 * 4 + m * 2, 2)].reshape(8, BLK, CG).astype(F32)
-                rows = pl.ds(pl.multiple_of(y2 * 128 + m * 64, 64), 64)
+                v = b1[g, jj].astype(F32)
                 for p in range(ROWS):
-                    act = gelu_value(v[:, p * QB:(p + 1) * QB, :].reshape(64, CG))
-                    ggate_o[0, p, rows, cols] = (gout[0, p, rows, cols].astype(F32) * act).astype(BF16)
-            return 0
-
-        lax.fori_loop(0, 2, step, 0)
-
-    for dy in range(FIRST):
-        gate_grad(dy)
-
-    def swap(dy):
-        rows = pl.ds(pl.multiple_of(((yy + 4 - dy) % 4) * 128, 128), 128)
+                    act = gelu_value(v[:, p * QB:(p + 1) * QB, :].reshape(32, CG))
+                    ggate_v[p, rows, cols] = (gout[p, rows, cols].astype(F32) * act).astype(BF16)
+            for p in range(ROWS):
+                pltpu.make_async_copy(ggate_v.at[p, rows], ggate_o.at[0, p, rows], l_sem.at[6]).start()
+            return 0
+
+        lax.fori_loop(0, 4, step, 0)
+
+    for e in range(FIRST):
+        gate_grad(e)
+
+    def swap(e):
         return pltpu.make_async_remote_copy(
-            src_ref=grp.at[1 - c, rows], dst_ref=cx.at[rows], send_sem=q_send.at[dy], recv_sem=q_recv.at[dy],
+            src_ref=grp.at[1 - c, e], dst_ref=cx.at[e], send_sem=q_send.at[e], recv_sem=q_recv.at[e],
             device_id={"outer": 1 - c}, device_id_type=MESH,
         )
 
-    def finish(dy):
-        swap(dy).wait()
-        y2 = (yy + 4 - dy) % 4
-
-        def step(m, _):
-            rows = pl.ds(pl.multiple_of(y2 * 128 + m * 32, 32), 32)
-            rs_s[y2 * 4 + m] = (grp[c, rows, :] + cx[rows, :]).astype(BF16)
-            return 0
-
-        lax.fori_loop(0, 4, step, 0)
-        scatter(rs_s, rs_r, 2, dy)
-
-    for dy in range(4):
-        wait_back(3, dy)
-        y2 = (yy + 4 - dy) % 4
-        rows = pl.ds(pl.multiple_of(y2 * 128, 128), 128)
+    def finish(e):
+        swap(e).wait()
+        for t in range(4):
+            rows = slice(t * 32, (t + 1) * 32)
+            rs_s[place(e, t, -1)] = (grp[c, e, rows, :] + cx[e, rows, :]).astype(BF16)
+        scatter(rs_s, rs_r, 2, e)
+
+    for e in range(4):
+        wait_back(3, e)
         for g in range(2):
             cols = slice(g * CG, (g + 1) * CG)
-            v = b2[g, pl.ds(y2 * 4, 4)].reshape(16, BLK, CG).astype(F32)
+            parts = [[], []]
+            for t in range(4):
+                jj = place(e, t, -1)
+                rows = pl.ds(pl.multiple_of(jj * 32, 32), 32)
+                v = b2[g, jj].astype(F32)
+                for p in range(ROWS):
+                    part = v[:, p * QB:(p + 1) * QB, :].reshape(32, CG).astype(BF16)
+                    gcb[p, rows, cols] = part
+                    parts[p].append(part)
             total = None
             for p in range(ROWS):
-                part = v[:, p * QB:(p + 1) * QB, :].reshape(128, CG).astype(BF16)
-                gcb[p, rows, cols] = part
-                term = dot(part, x[0, p, :, cols], 1, 1)
+                term = dot(jnp.concatenate(parts[p], axis=0), x[p, :, cols], 1, 1)
                 total = term if total is None else total + term
-            grp[g, rows, :] = total
-        swap(dy).start()
-        if dy > 0:
-            finish(dy - 1)
+            grp[g, e] = total
+        swap(e).start()
+        if e > 0:
+            finish(e - 1)
     finish(3)
     rs_r[j] = rs_s[j]
-    for dy in range(SECOND, THIRD):
-        send_back(t1, b1, 2, dy)
+    for e in range(SECOND, THIRD):
+        send_back(t1, b1, 2, e)
 
     def input_grad(m, _):
         rows = pl.ds(pl.multiple_of(m * 128, 128), 128)
         for g in range(2):
             cols = slice(g * CG, (g + 1) * CG)
             for p in range(ROWS):
-                gin_o[0, p, rows, cols] = dot(rt[g, rows, :], gcb[p, :, cols], 1, 0).astype(BF16)
+                gin_v[p, rows, cols] = dot(rt[g, rows, :], gcb[p, :, cols], 1, 0).astype(BF16)
         return 0
 
     lax.fori_loop(0, 4, input_grad, 0)
+    gin_out = pltpu.make_async_copy(gin_v, gin_o.at[0], l_sem.at[5])
+    gin_out.start()
 
     wait_bytes(ls_r.at[pl.ds(0, XY - 1)], m_recv.at[0])
     wait_bytes(rs_r.at[pl.ds(0, XY - 1)], m_recv.at[2])
@@ -314,10 +336,10 @@
     def _():
         to_z(0).start()
 
-    for dy in range(THIRD, 4):
-        send_back(t1, b1, 2, dy)
-    for dy in range(FIRST, SECOND):
-        gate_grad(dy)
+    for e in range(THIRD, 4):
+        send_back(t1, b1, 2, e)
+    for e in range(FIRST, SECOND):
+        gate_grad(e)
 
     @pl.when(d == c)
     def _():
@@ -338,8 +360,8 @@
 
         lax.fori_loop(1, XY, give, 0)
 
-    for dy in range(SECOND, 4):
-        gate_grad(dy)
+    for e in range(SECOND, 4):
+        gate_grad(e)
 
     @pl.when(d == c)
     def _():
@@ -359,18 +381,28 @@
         wait_bytes(fin, m_recv.at[5])
 
     for k in range(XY):
-        gr_o[0, k * 32:(k + 1) * 32, 0:256] = fin[k, 0:32, :].astype(F32)
-        gr_o[0, k * 32:(k + 1) * 32, 256:512] = fin[k, 32:64, :].astype(F32)
-        gl_o[0, k * 16:(k + 1) * 16, :] = fin[k, 64:80, :].astype(F32)
-
+        gr_v[k * 32:(k + 1) * 32, 0:256] = fin[k, 0:32, :].astype(F32)
+        gr_v[k * 32:(k + 1) * 32, 256:512] = fin[k, 32:64, :].astype(F32)
+        gl_v[k * 16:(k + 1) * 16, :] = fin[k, 64:80, :].astype(F32)
+
+    outs = (
+        pltpu.make_async_copy(gr_v, gr_o.at[0], l_sem.at[7]),
+        pltpu.make_async_copy(gl_v, gl_o.at[0], l_sem.at[8]),
+    )
+    for out in outs:
+        out.start()
     for n in range(4):
         wait_bytes(r1.at[pl.ds(0, PEERS - 1)], a_send.at[n])
     wait_bytes(ls_r.at[pl.ds(0, XY - 1)], m_send.at[0])
     wait_bytes(rs_r.at[pl.ds(0, XY - 1)], m_send.at[2])
+    wait_bytes(ggate_v, l_sem.at[6])
+    gin_out.wait()
+    for out in outs:
+        out.wait()
 
 
 def body(inputs, gate_in, grad_out, right_factor, left_factor):
-    vmem = pl.BlockSpec(memory_space=pltpu.VMEM)
+    hbm = pl.BlockSpec(memory_space=pl.ANY)
     out_shape = (
         jax.ShapeDtypeStruct((1, ROWS, Q, 2 * CG), BF16),
         jax.ShapeDtypeStruct((1, ROWS, Q, 2 * CG), BF16),
@@ -386,15 +418,25 @@
         pltpu.VMEM((PEERS, BLK, CG), BF16),
         pltpu.VMEM((2, XY, ZH, BLK, CG), BF16),
         pltpu.VMEM((2, XY, ZH, BLK, CG), BF16),
+        pltpu.VMEM((ROWS, Q, 2 * CG), BF16),
+        pltpu.VMEM((ROWS, Q, 2 * CG), BF16),
+        pltpu.VMEM((ROWS, Q, 2 * CG), BF16),
+        pltpu.VMEM((2, Q, Q), BF16),
+        pltpu.VMEM((2, P_ALL, P_ALL), BF16),
+        pltpu.VMEM((ROWS, Q, 2 * CG), BF16),
+        pltpu.VMEM((ROWS, Q, 2 * CG), BF16),
+        pltpu.VMEM((Q, Q), F32),
+        pltpu.VMEM((P_ALL, P_ALL), F32),
         pltpu.VMEM((LANES, PEERS * BLK, 128), F32),
         pltpu.VMEM((LANES, PEERS * BLK, 128), F32),
         pltpu.VMEM((QB, P_ALL, CG), F32),
         pltpu.VMEM((QB, P_ALL, CG), BF16),
+        pltpu.VMEM((QB, P_ALL, CG), BF16),
         pltpu.VMEM((ROWS, Q, 2 * CG), BF16),
         pltpu.VMEM((2, Q, Q), BF16),
         pltpu.VMEM((P_ALL, P_ALL), BF16),
-        pltpu.VMEM((2, Q, Q), F32),
-        pltpu.VMEM((Q, Q), F32),
+        pltpu.VMEM((2, 4, 128, Q), F32),
+        pltpu.VMEM((4, 128, Q), F32),
         pltpu.VMEM((XY, 32, Q), BF16),
         pltpu.VMEM((XY, 32, Q), BF16),
         pltpu.VMEM((XY, 16, P_ALL), BF16),
@@ -408,12 +450,13 @@
         pltpu.SemaphoreType.DMA((6,)),
         pltpu.SemaphoreType.DMA((4,)),
         pltpu.SemaphoreType.DMA((4,)),
+        pltpu.SemaphoreType.DMA((9,)),
     ]
     return pl.pallas_call(
         kernel,
         out_shape=out_shape,
-        in_specs=[vmem] * 5,
-        out_specs=(vmem,) * 4,
+        in_specs=[hbm] * 5,
+        out_specs=(hbm,) * 4,
         scratch_shapes=scratch,
         compiler_params=pltpu.CompilerParams(
             collective_id=0, has_side_effects=True, vmem_limit_bytes=56 * 1024 * 1024

time: 184 us -> 175 us (0.951)
  Pallas kernels: 177 us -> 168 us
    pallas_call x1, Pallas kernels: 177 us -> 168 us  [body(): pl.pallas_call(kernel, out_shape=out_shape, in_specs=[hbm] * 5, out_specs...]
where the time goes in v2:
time: 175 us
  Pallas kernels  168 us (96%)
  local copies, waits for them, and re-layouts  6.36 us (4%)
    pallas_call x1, Pallas kernels, body(): pl.pallas_call(kernel, out_shape=out_shape, in_specs=[hbm] * 5, out_specs...  168 us
    unnamed x10, local copies, waits for them, and re-layouts  6.36 us

profile of v2, /device:TPU:1, one launch (start us, length us, event | category | flops | bytes accessed | tf_op | source)
XLA Modules:
  0.0 175.2 jit_solution(17287117310937434382)
XLA Ops:
  0.6 168.2 %shard_map.84 = (bf16[1,2,512,768]{3,2,1,0:T(8,128)(2,1)}, bf16[1,2,512,768]{3,2,1,0:T(8,128)(2,1)}, f32[1,512,512]{2,1,0:T(8,128)}, f32[1,256,256]{2,1,0:T(8,128)}) custom-call(bf16[1,2,512,768]{3,2,1,0:T(8,128)(2,1)} %x_h.1, bf16[1,2,512,768]{3,2,1,0:T(8,128)(2,1)} %gate_h.1, bf16[1,2,512,768]{3,2,1,0:T(8,128)(2,1)} %gout_h.1, bf16[2,512,512]{2,1,0:T(8,128)(2,1)} %rf_h.1, ...), custom_call_target="tpu_custom_call" | custom-call | flops 4000000000 | bytes 12000000 | tf_op jit(solution)/shard_map/pallas_call | solution.py:455
  168.9 0.0 copy-start
  168.9 2.8 %copy.13 = bf16[1,2,512,768]{3,2,1,0:T(8,128)(2,1)} copy(bf16[1,2,512,768]{3,2,1,0:T(8,128)(2,1)} %get-tuple-element.8) | data formatting | bytes 3145728
  171.7 0.0 copy-done
  171.7 0.0 copy-start.1
  171.7 1.1 copy.14
  172.8 0.6 copy-done.1
  173.5 0.0 copy-start.2
  173.5 1.0 copy.15
  174.4 0.1 copy-done.2
  174.5 0.7 copy.16
Async XLA Ops:
  168.9 2.8 %copy-start = (bf16[1,2,512,768]{3,2,1,0:T(8,128)(2,1)S(1)}, bf16[1,2,512,768]{3,2,1,0:T(8,128)(2,1)}, u32[]{:S(2)}) copy-start(bf16[1,2,512,768]{3,2,1,0:T(8,128)(2,1)} %get-tuple-element.9) | copy-start | bytes 4718596
  171.7 1.8 %copy-start.1 = (f32[1,512,512]{2,1,0:T(8,128)S(1)}, f32[1,512,512]{2,1,0:T(8,128)}, u32[]{:S(2)}) copy-start(f32[1,512,512]{2,1,0:T(8,128)} %get-tuple-element.10) | copy-start | bytes 3145732
  173.5 1.1 copy-start.2

commit v3 on v2

v3 whole, which is shorter than its diff:
```python
import jax
import jax.numpy as jnp
from jax import lax
from jax.experimental import pallas as pl
from jax.experimental.pallas import tpu as pltpu
from jax.sharding import PartitionSpec as P

MESH = pl.DeviceIdType.MESH
F32 = jnp.float32
BF16 = jnp.bfloat16

INNER = 64
ZH = 4
XY = 16
ROWS = 2
CHIP = 4
CG = 384
LANES = CG // 128
Q = 512
P_ALL = 256
QB = 8
BLK = CHIP * QB
FIRST, SECOND, THIRD = 1, 2, 3


def gelu_value(mixed):
    return mixed * (0.5 * (1.0 + lax.erf(mixed * 0.7071067811865476)))


def gelu_slope(mixed):
    normal_cdf = 0.5 * (1.0 + lax.erf(mixed * 0.7071067811865476))
    density = jnp.exp(-0.5 * mixed * mixed) * 0.3989422804014327
    return normal_cdf + mixed * density


def wait_bytes(ref, sem):
    pltpu.make_async_copy(ref, ref, sem).wait()


def dot(a, b, ca, cb):
    return lax.dot_general(a, b, (((ca,), (cb,)), ((), ())), preferred_element_type=F32)


def kernel(
    x_h, gate_h, gout_h, rf_h, lf_h,
    gin_o, ggate_o, gr_o, gl_o,
    s1, s2, r1, r2, t1, t2, b1, b2,
    x, gate, gout, rf, lf, gin_v, ggate_v, gr_v, gl_v,
    wide_a, wide_b, wide_c, colsb, gmb, gcb, rt, lt,
    rs_s, rs_r, ls_s, ls_r, share, zrecv, fin,
    a_send, a_recv, m_send, m_recv, e_send, e_recv, l_sem,
):
    i = lax.axis_index("inner")
    c = lax.axis_index("outer")
    d = lax.axis_index("dp")
    zh = i % ZH
    j = i // ZH
    ys = [(j // 4 + n) % 4 for n in range(4)]
    xs = [(j % 4 + n) % 4 for n in range(4)]
    mine = pl.ds(pl.multiple_of(c * CG, CG), CG)
    theirs = pl.ds(pl.multiple_of((1 - c) * CG, CG), CG)
    my_rows = pl.ds(c * ROWS, ROWS)
    their_rows = pl.ds((1 - c) * ROWS, ROWS)

    def place(e, t, sign):
        return ys[sign * (e + t) % 4] * 4 + xs[sign * t % 4]

    def source(e, t):
        return lax.rem(ys[0] + 8 - e - t, 4) * 4 + lax.rem(xs[0] + 4 - t, 4)

    def each_partner(e, act):
        if e == 0:
            for t in range(1, 4):
                act(place(e, t, 1) * ZH + (zh + t) % ZH)

        def step(u, _):
            for t in range(4):
                act(place(e, t, 1) * ZH + lax.rem(zh + t + u, ZH))
            return 0

        lax.fori_loop(1 if e == 0 else 0, ZH, step, 0)

    arrays = ((x_h, x), (gate_h, gate), (gout_h, gout))
    loads = [
        pltpu.make_async_copy(src.at[0, :, :, mine], dst.at[my_rows], l_sem.at[n])
        for n, (src, dst) in enumerate(arrays)
    ]
    loads.append(pltpu.make_async_copy(rf_h.at[c], rf, l_sem.at[3]))
    loads.append(pltpu.make_async_copy(lf_h.at[c], lf, l_sem.at[4]))
    for n in (0, 3, 1, 2, 4):
        loads[n].start()

    barrier = pltpu.get_barrier_semaphore()

    def greet(ii):
        pl.semaphore_signal(barrier, inc=1, device_id={"inner": ii}, device_id_type=MESH)

    pl.semaphore_signal(barrier, inc=1, device_id={"outer": 1 - c}, device_id_type=MESH)
    for e in range(4):
        each_partner(e, greet)
    for k in range(ZH):
        pl.semaphore_signal(
            barrier, inc=1, device_id={"inner": j * ZH + (zh + k) % ZH, "dp": 1 - d}, device_id_type=MESH
        )

    def right_mix(h):
        def step(m, _):
            lhs = rf[pl.ds(pl.multiple_of(m * 128, 128), 128), :]
            parts = [dot(lhs, x[h * ROWS + p], 1, 0).reshape(16, QB, CG) for p in range(ROWS)]
            half = pl.ds(pl.multiple_of(h * 16, 16), 16)
            s1[pl.ds(m * 16, 16), half, :] = jnp.concatenate(parts, axis=1).astype(BF16)
            return 0

        lax.fori_loop(0, 4, step, 0)

    loads[0].wait()
    loads[3].wait()
    right_mix(c)

    pl.semaphore_wait(barrier, INNER + ZH)
    gifts = [
        pltpu.make_async_remote_copy(
            src_ref=src.at[0, :, :, theirs], dst_ref=dst.at[my_rows], send_sem=e_send.at[n], recv_sem=e_recv.at[n],
            device_id={"outer": 1 - c}, device_id_type=MESH,
        )
        for n, (src, dst) in enumerate(arrays)
    ]
    for gift in gifts:
        gift.start()

    def weigh(e):
        for t in range(4):
            jj = place(e, t, 1)
            rows = pl.ds(pl.multiple_of(jj * 32, 32), 32)
            parts = []
            for p in range(CHIP):
                a = gout[p, rows, :].astype(F32)
                b = gate[p, rows, :].astype(F32)
                parts.append((a * b).reshape(4, QB, CG))
            s2[pl.ds(jj * 4, 4)] = jnp.concatenate(parts, axis=1).astype(BF16)

    def send(src, dst, n, sem, e):
        def act(ii):
            pltpu.make_async_remote_copy(
                src_ref=src.at[ii], dst_ref=dst.at[i], send_sem=a_send.at[n], recv_sem=a_recv.at[sem],
                device_id={"inner": ii}, device_id_type=MESH,
            ).start()

        each_partner(e, act)

    def send_chunk(src, dst, n, e):
        send(src, dst, n, 4 * n - 3 + e, e)

    def wait_chunk(n, e):
        wait_bytes(t1.at[pl.ds(0, 15 if e == 0 else 16)], a_recv.at[4 * n - 3 + e])

    gifts[0].wait_recv()
    right_mix(1 - c)
    for e in range(4):
        send(s1, r1, 0, 0, e)
    loads[1].wait()
    loads[2].wait()
    gifts[1].wait_recv()
    gifts[2].wait_recv()
    for e in range(4):
        weigh(e)
        send_chunk(s2, r2, 1, e)
    r1[i] = s1[i]
    r2[i] = s2[i]
    loads[4].wait()
    lt[...] = lf[...].astype(F32).T.astype(BF16)
    for h in range(2):
        rt[:, h * 256:(h + 1) * 256] = rf[h * 256:(h + 1) * 256, :].astype(F32).T.astype(BF16)

    def column(q):
        return jnp.concatenate([wide_a[n, pl.ds(q, P_ALL, stride=QB), :] for n in range(LANES)], axis=1)

    wait_bytes(t1.at[pl.ds(0, INNER - 1)], a_recv.at[0])

    def widen(m, _):
        v = r1[pl.ds(m * 4, 4)].reshape(128, CG).astype(F32)
        for n in range(LANES):
            wide_a[n, pl.ds(pl.multiple_of(m * 128, 128), 128), :] = v[:, n * 128:(n + 1) * 128]
        return 0

    lax.fori_loop(0, XY, widen, 0)
    for q in range(QB):
        xq = column(q).astype(BF16)
        colsb[q] = xq
        mixed = dot(lf[...], xq, 1, 0)
        for n in range(LANES):
            wide_b[n, pl.ds(q, P_ALL, stride=QB), :] = mixed[:, n * 128:(n + 1) * 128]

    def narrow(m, _):
        for n in range(LANES):
            v = wide_b[n, pl.ds(pl.multiple_of(m * 64, 64), 64), :].astype(BF16)
            t1[pl.ds(m * 2, 2), :, n * 128:(n + 1) * 128] = v.reshape(2, BLK, 128)
        return 0

    lax.fori_loop(0, 32, narrow, 0)
    b1[i] = t1[i]
    for e in range(FIRST):
        send_chunk(t1, b1, 2, e)

    def slopes(m, _):
        rows = pl.ds(pl.multiple_of(m * 64, 64), 64)
        for n in range(LANES):
            wide_b[n, rows, :] = gelu_slope(wide_b[n, rows, :])
        return 0

    lax.fori_loop(0, 32, slopes, 0)

    for e in range(4):
        wait_chunk(1, e)
        for t in range(4):
            jj = place(e, t, -1)
            rows = pl.ds(pl.multiple_of(jj * 128, 128), 128)
            v = r2[pl.ds(jj * 4, 4)].reshape(128, CG).astype(F32)
            for n in range(LANES):
                wide_a[n, rows, :] = v[:, n * 128:(n + 1) * 128] * wide_b[n, rows, :]
    for q in range(QB):
        gmb[q] = column(q).astype(BF16)

    for e in range(4):
        spots = [place(e, t, 1) for t in range(4)]
        lhs = jnp.concatenate([lt[pl.ds(pl.multiple_of(jj * 16, 16), 16), :] for jj in spots], axis=0)
        for q in range(QB):
            v = dot(lhs, gmb[q], 1, 0)
            for t, jj in enumerate(spots):
                for n in range(LANES):
                    wide_c[n, pl.ds(jj * 128 + q, 16, stride=QB), :] = v[t * 16:(t + 1) * 16, n * 128:(n + 1) * 128]
        for jj in spots:
            rows = pl.ds(pl.multiple_of(jj * 128, 128), 128)
            for n in range(LANES):
                v = wide_c[n, rows, :].astype(BF16)
                t2[pl.ds(jj * 4, 4), :, n * 128:(n + 1) * 128] = v.reshape(4, BLK, 128)
        send_chunk(t2, b2, 3, e)
    b2[i] = t2[i]
    for e in range(FIRST, SECOND):
        send_chunk(t1, b1, 2, e)
    gl_acc = jnp.zeros((P_ALL, P_ALL), F32)
    for q in range(QB):
        gl_acc = gl_acc + dot(gmb[q], colsb[q], 1, 1)
    ls_s[...] = gl_acc.astype(BF16).reshape(XY, 16, P_ALL)

    def scatter(src, dst, n, e):
        for t in range(1 if e == 0 else 0, 4):
            jj = place(e, t, -1)
            pltpu.make_async_remote_copy(
                src_ref=src.at[jj], dst_ref=dst.at[j], send_sem=m_send.at[n], recv_sem=m_recv.at[n],
                device_id={"inner": jj * ZH + zh}, device_id_type=MESH,
            ).start()

    for e in range(4):
        scatter(ls_s, ls_r, 0, e)
    ls_r[j] = ls_s[j]

    def hand_out(src, dst, rows, n):
        pltpu.make_async_copy(src.at[my_rows, rows], dst.at[0, :, rows, mine], l_sem.at[n]).start()
        pltpu.make_async_remote_copy(
            src_ref=src.at[their_rows, rows], dst_ref=dst.at[0, :, rows, mine],
            send_sem=e_send.at[n], recv_sem=e_recv.at[n],
            device_id={"outer": 1 - c}, device_id_type=MESH,
        ).start()

    def gate_grad(e):
        wait_chunk(2, e)

        def step(t, _):
            jj = source(e, t)
            rows = pl.ds(pl.multiple_of(jj * 32, 32), 32)
            v = b1[pl.ds(jj * 4, 4)].astype(F32)
            for p in range(CHIP):
                act = gelu_value(v[:, p * QB:(p + 1) * QB, :].reshape(32, CG))
                ggate_v[p, rows, :] = (gout[p, rows, :].astype(F32) * act).astype(BF16)
            hand_out(ggate_v, ggate_o, rows, 6)
            return 0

        lax.fori_loop(0, 4, step, 0)

    for e in range(FIRST):
        gate_grad(e)

    for e in range(4):
        wait_chunk(3, e)
        spots = [place(e, t, -1) for t in range(4)]
        parts = [[] for _ in range(CHIP)]
        for jj in spots:
            rows = pl.ds(pl.multiple_of(jj * 32, 32), 32)
            v = b2[pl.ds(jj * 4, 4)].astype(F32)
            for p in range(CHIP):
                part = v[:, p * QB:(p + 1) * QB, :].reshape(32, CG).astype(BF16)
                gcb[p, rows, :] = part
                parts[p].append(part)
        total = None
        for p in range(CHIP):
            term = dot(jnp.concatenate(parts[p], axis=0), x[p], 1, 1)
            total = term if total is None else total + term
        for t, jj in enumerate(spots):
            rs_s[jj] = total[t * 32:(t + 1) * 32, :].astype(BF16)
        scatter(rs_s, rs_r, 1, e)
    rs_r[j] = rs_s[j]
    for e in range(SECOND, THIRD):
        send_chunk(t1, b1, 2, e)

    def input_grad(m, _):
        rows = pl.ds(pl.multiple_of(m * 128, 128), 128)
        for p in range(CHIP):
            gin_v[p, rows, :] = dot(rt[rows, :], gcb[p], 1, 0).astype(BF16)
        hand_out(gin_v, gin_o, rows, 5)
        return 0

    lax.fori_loop(0, 4, input_grad, 0)

    wait_bytes(ls_r.at[pl.ds(0, XY - 1)], m_recv.at[0])
    wait_bytes(rs_r.at[pl.ds(0, XY - 1)], m_recv.at[1])
    gr_sum = rs_r[0].astype(F32)
    gl_sum = ls_r[0].astype(F32)
    for k in range(1, XY):
        gr_sum = gr_sum + rs_r[k].astype(F32)
        gl_sum = gl_sum + ls_r[k].astype(F32)
    share[0:32, :] = gr_sum[:, 0:256].astype(BF16)
    share[32:64, :] = gr_sum[:, 256:512].astype(BF16)
    share[64:80, :] = gl_sum.astype(BF16)

    def to_z(k):
        return pltpu.make_async_remote_copy(
            src_ref=share, dst_ref=zrecv.at[zh * 2 + d], send_sem=m_send.at[2], recv_sem=m_recv.at[2],
            device_id={"inner": j * ZH + (zh + k) % ZH, "dp": c}, device_id_type=MESH,
        )

    for k in range(1, ZH):
        to_z(k).start()

    @pl.when(d != c)
    def _():
        to_z(0).start()

    for e in range(THIRD, 4):
        send_chunk(t1, b1, 2, e)
    for e in range(FIRST, SECOND):
        gate_grad(e)

    @pl.when(d == c)
    def _():
        zrecv[zh * 2 + d] = share[...]
        wait_bytes(zrecv.at[pl.ds(0, 7)], m_recv.at[2])
        total = zrecv[0].astype(F32)
        for k in range(1, 8):
            total = total + zrecv[k].astype(F32)
        fin[j] = total.astype(BF16)

        def give(k, _):
            jj = (j + k) % XY
            pltpu.make_async_remote_copy(
                src_ref=fin.at[j], dst_ref=fin.at[j], send_sem=m_send.at[3], recv_sem=m_recv.at[3],
                device_id={"inner": jj * ZH + zh}, device_id_type=MESH,
            ).start()
            return 0

        lax.fori_loop(1, XY, give, 0)

    for e in range(SECOND, 4):
        gate_grad(e)

    @pl.when(d == c)
    def _():
        wait_bytes(fin.at[pl.ds(0, XY - 1)], m_recv.at[3])
        pltpu.make_async_remote_copy(
            src_ref=fin, dst_ref=fin, send_sem=m_send.at[4], recv_sem=m_recv.at[4],
            device_id={"outer": 1 - c}, device_id_type=MESH,
        ).start()
        wait_bytes(fin.at[pl.ds(0, XY - 1)], m_send.at[3])
        wait_bytes(zrecv.at[pl.ds(0, 3)], m_send.at[2])
        wait_bytes(fin, m_send.at[4])

    @pl.when(d != c)
    def _():
        wait_bytes(zrecv.at[pl.ds(0, 4)], m_send.at[2])
        wait_bytes(fin, m_recv.at[4])

    for k in range(XY):
        gr_v[k * 32:(k + 1) * 32, 0:256] = fin[k, 0:32, :].astype(F32)
        gr_v[k * 32:(k + 1) * 32, 256:512] = fin[k, 32:64, :].astype(F32)
        gl_v[k * 16:(k + 1) * 16, :] = fin[k, 64:80, :].astype(F32)

    outs = (
        pltpu.make_async_copy(gr_v, gr_o.at[0], l_sem.at[7]),
        pltpu.make_async_copy(gl_v, gl_o.at[0], l_sem.at[8]),
    )
    for out in outs:
        out.start()
    for n in range(4):
        wait_bytes(t1.at[pl.ds(0, INNER - 1)], a_send.at[n])
    wait_bytes(ls_r.at[pl.ds(0, XY - 1)], m_send.at[0])
    wait_bytes(rs_r.at[pl.ds(0, XY - 1)], m_send.at[1])
    for gift in gifts:
        gift.wait_send()
    half = ggate_v.at[pl.ds(0, ROWS)]
    for n in (5, 6):
        wait_bytes(half, l_sem.at[n])
        wait_bytes(half, e_send.at[n])
        wait_bytes(half, e_recv.at[n])
    for out in outs:
        out.wait()


def body(inputs, gate_in, grad_out, right_factor, left_factor):
    hbm = pl.BlockSpec(memory_space=pl.ANY)
    out_shape = (
        jax.ShapeDtypeStruct((1, ROWS, Q, 2 * CG), BF16),
        jax.ShapeDtypeStruct((1, ROWS, Q, 2 * CG), BF16),
        jax.ShapeDtypeStruct((1, Q, Q), F32),
        jax.ShapeDtypeStruct((1, P_ALL, P_ALL), F32),
    )
    blocks = pltpu.VMEM((INNER, BLK, CG), BF16)
    rows = pltpu.VMEM((CHIP, Q, CG), BF16)
    wide = pltpu.VMEM((LANES, INNER * BLK, 128), F32)
    columns = pltpu.VMEM((QB, P_ALL, CG), BF16)
    scratch = [blocks] * 8 + [
        rows, rows, rows,
        pltpu.VMEM((Q, Q), BF16),
        pltpu.VMEM((P_ALL, P_ALL), BF16),
        rows, rows,
        pltpu.VMEM((Q, Q), F32),
        pltpu.VMEM((P_ALL, P_ALL), F32),
        wide, wide, wide,
        columns, columns,
        rows,
        pltpu.VMEM((Q, Q), BF16),
        pltpu.VMEM((P_ALL, P_ALL), BF16),
        pltpu.VMEM((XY, 32, Q), BF16),
        pltpu.VMEM((XY, 32, Q), BF16),
        pltpu.VMEM((XY, 16, P_ALL), BF16),
        pltpu.VMEM((XY, 16, P_ALL), BF16),
        pltpu.VMEM((80, 256), BF16),
        pltpu.VMEM((8, 80, 256), BF16),
        pltpu.VMEM((XY, 80, 256), BF16),
        pltpu.SemaphoreType.DMA((4,)),
        pltpu.SemaphoreType.DMA((13,)),
        pltpu.SemaphoreType.DMA((5,)),
        pltpu.SemaphoreType.DMA((5,)),
        pltpu.SemaphoreType.DMA((7,)),
        pltpu.SemaphoreType.DMA((7,)),
        pltpu.SemaphoreType.DMA((9,)),
    ]
    return pl.pallas_call(
        kernel,
        out_shape=out_shape,
        in_specs=[hbm] * 5,
        out_specs=(hbm,) * 4,
        scratch_shapes=scratch,
        compiler_params=pltpu.CompilerParams(
            collective_id=0, has_side_effects=True, vmem_limit_bytes=48 * 1024 * 1024
        ),
        cost_estimate=pl.CostEstimate(flops=4 * 10**9, bytes_accessed=12 * 10**6, transcendentals=3 * 10**6),
    )(inputs, gate_in, grad_out, right_factor, left_factor)


def solution(mesh):
    rows = P("dp", ("inner", "outer"), None, None)
    return jax.shard_map(
        body,
        mesh=mesh,
        in_specs=(rows, rows, rows, P(), P()),
        out_specs=(rows, rows, P("dp", None, None), P("dp", None, None)),
        check_vma=False,
    )
```

time: 175 us -> 175 us (level)
    unnamed x10 -> x8, local copies, waits for them, and re-layouts: 6.36 us -> 6.13 us
where the time goes in v3:
time: 175 us
  Pallas kernels  168 us (96%)
  local copies, waits for them, and re-layouts  6.13 us (4%)
    pallas_call x1, Pallas kernels, body(): pl.pallas_call(kernel, out_shape=out_shape, in_specs=[hbm] * 5, out_specs...  168 us
    unnamed x8, local copies, waits for them, and re-layouts  6.13 us

profile of v3, /device:TPU:1, one launch (start us, length us, event | category | flops | bytes accessed | tf_op | source)
XLA Modules:
  0.0 175.2 jit_solution(4629261017370429489)
XLA Ops:
  0.6 0.0 copy-start
  0.6 1.2 copy-done
  1.9 0.0 copy-start.1
  1.9 0.9 copy-done.1
  2.8 168.5 %shard_map.84 = (bf16[1,2,512,768]{3,2,1,0:T(8,128)(2,1)S(1)}, bf16[1,2,512,768]{3,2,1,0:T(8,128)(2,1)S(1)}, f32[1,512,512]{2,1,0:T(8,128)S(1)}, f32[1,256,256]{2,1,0:T(8,128)S(1)}) custom-call(bf16[1,2,512,768]{3,2,1,0:T(8,128)(2,1)} %x_h.1, bf16[1,2,512,768]{3,2,1,0:T(8,128)(2,1)} %gate_h.1, bf16[1,2,512,768]{3,2,1,0:T(8,128)(2,1)} %gout_h.1, ...), custom_call_target="tpu_custom_call" | custom-call | flops 4000000000 | bytes 12000000 | tf_op jit(solution)/shard_map/pallas_call | solution.py:447
  171.3 1.1 copy.13
  172.4 1.1 copy.14
  173.6 1.0 copy.15
  174.5 0.7 copy.16
Async XLA Ops:
  0.6 1.2 copy-start
  1.9 0.9 copy-start.1

commit v4 on v3

--- a/solution.py
+++ b/solution.py
@@ -20,7 +20,12 @@
 P_ALL = 256
 QB = 8
 BLK = CHIP * QB
-FIRST, SECOND, THIRD = 1, 2, 3
+
+BEFORE_COLS = (0, 1)
+AFTER_COLS = (2,)
+AFTER_PLANE = (3,)
+AFTER_Z = (4, 5)
+AFTER_SHARES = (6, 7)
 
 
 def gelu_value(mixed):
@@ -45,7 +50,7 @@
     x_h, gate_h, gout_h, rf_h, lf_h,
     gin_o, ggate_o, gr_o, gl_o,
     s1, s2, r1, r2, t1, t2, b1, b2,
-    x, gate, gout, rf, lf, gin_v, ggate_v, gr_v, gl_v,
+    x, gate, gout, rf, lf, gin_v, ggate_v,
     wide_a, wide_b, wide_c, colsb, gmb, gcb, rt, lt,
     rs_s, rs_r, ls_s, ls_r, share, zrecv, fin,
     a_send, a_recv, m_send, m_recv, e_send, e_recv, l_sem,
@@ -68,17 +73,18 @@
     def source(e, t):
         return lax.rem(ys[0] + 8 - e - t, 4) * 4 + lax.rem(xs[0] + 4 - t, 4)
 
-    def each_partner(e, act):
-        if e == 0:
+    def each_partner(e, act, first=0, last=ZH):
+        if e == 0 and first == 0:
             for t in range(1, 4):
                 act(place(e, t, 1) * ZH + (zh + t) % ZH)
+            first = 1
 
         def step(u, _):
             for t in range(4):
                 act(place(e, t, 1) * ZH + lax.rem(zh + t + u, ZH))
             return 0
 
-        lax.fori_loop(1 if e == 0 else 0, ZH, step, 0)
+        lax.fori_loop(first, last, step, 0)
 
     arrays = ((x_h, x), (gate_h, gate), (gout_h, gout))
     loads = [
@@ -125,8 +131,7 @@
         )
         for n, (src, dst) in enumerate(arrays)
     ]
-    for gift in gifts:
-        gift.start()
+    gifts[0].start()
 
     def weigh(e):
         for t in range(4):
@@ -139,22 +144,28 @@
                 parts.append((a * b).reshape(4, QB, CG))
             s2[pl.ds(jj * 4, 4)] = jnp.concatenate(parts, axis=1).astype(BF16)
 
-    def send(src, dst, n, sem, e):
+    def send(src, dst, n, sem, e, first=0, last=ZH):
         def act(ii):
             pltpu.make_async_remote_copy(
                 src_ref=src.at[ii], dst_ref=dst.at[i], send_sem=a_send.at[n], recv_sem=a_recv.at[sem],
                 device_id={"inner": ii}, device_id_type=MESH,
             ).start()
 
-        each_partner(e, act)
+        each_partner(e, act, first, last)
 
     def send_chunk(src, dst, n, e):
         send(src, dst, n, 4 * n - 3 + e, e)
 
+    def send_mixed(*pieces):
+        for k in pieces:
+            send(t1, b1, 2, 5 + k // 2, k // 2, k % 2 * 2, k % 2 * 2 + 2)
+
     def wait_chunk(n, e):
         wait_bytes(t1.at[pl.ds(0, 15 if e == 0 else 16)], a_recv.at[4 * n - 3 + e])
 
     gifts[0].wait_recv()
+    gifts[1].start()
+    gifts[2].start()
     right_mix(1 - c)
     for e in range(4):
         send(s1, r1, 0, 0, e)
@@ -199,8 +210,7 @@
 
     lax.fori_loop(0, 32, narrow, 0)
     b1[i] = t1[i]
-    for e in range(FIRST):
-        send_chunk(t1, b1, 2, e)
+    send_mixed(*BEFORE_COLS)
 
     def slopes(m, _):
         rows = pl.ds(pl.multiple_of(m * 64, 64), 64)
@@ -236,8 +246,7 @@
                 t2[pl.ds(jj * 4, 4), :, n * 128:(n + 1) * 128] = v.reshape(4, BLK, 128)
         send_chunk(t2, b2, 3, e)
     b2[i] = t2[i]
-    for e in range(FIRST, SECOND):
-        send_chunk(t1, b1, 2, e)
+    send_mixed(*AFTER_COLS)
     gl_acc = jnp.zeros((P_ALL, P_ALL), F32)
     for q in range(QB):
         gl_acc = gl_acc + dot(gmb[q], colsb[q], 1, 1)
@@ -278,8 +287,7 @@
 
         lax.fori_loop(0, 4, step, 0)
 
-    for e in range(FIRST):
-        gate_grad(e)
+    gate_grad(0)
 
     for e in range(4):
         wait_chunk(3, e)
@@ -300,8 +308,7 @@
             rs_s[jj] = total[t * 32:(t + 1) * 32, :].astype(BF16)
         scatter(rs_s, rs_r, 1, e)
     rs_r[j] = rs_s[j]
-    for e in range(SECOND, THIRD):
-        send_chunk(t1, b1, 2, e)
+    send_mixed(*AFTER_PLANE)
 
     def input_grad(m, _):
         rows = pl.ds(pl.multiple_of(m * 128, 128), 128)
@@ -336,10 +343,8 @@
     def _():
         to_z(0).start()
 
-    for e in range(THIRD, 4):
-        send_chunk(t1, b1, 2, e)
-    for e in range(FIRST, SECOND):
-        gate_grad(e)
+    send_mixed(*AFTER_Z)
+    gate_grad(1)
 
     @pl.when(d == c)
     def _():
@@ -360,8 +365,8 @@
 
         lax.fori_loop(1, XY, give, 0)
 
-    for e in range(SECOND, 4):
-        gate_grad(e)
+    send_mixed(*AFTER_SHARES)
+    gate_grad(2)
 
     @pl.when(d == c)
     def _():
@@ -380,16 +385,11 @@
         wait_bytes(fin, m_recv.at[4])
 
     for k in range(XY):
-        gr_v[k * 32:(k + 1) * 32, 0:256] = fin[k, 0:32, :].astype(F32)
-        gr_v[k * 32:(k + 1) * 32, 256:512] = fin[k, 32:64, :].astype(F32)
-        gl_v[k * 16:(k + 1) * 16, :] = fin[k, 64:80, :].astype(F32)
-
-    outs = (
-        pltpu.make_async_copy(gr_v, gr_o.at[0], l_sem.at[7]),
-        pltpu.make_async_copy(gl_v, gl_o.at[0], l_sem.at[8]),
-    )
-    for out in outs:
-        out.start()
+        gr_o[0, k * 32:(k + 1) * 32, 0:256] = fin[k, 0:32, :].astype(F32)
+        gr_o[0, k * 32:(k + 1) * 32, 256:512] = fin[k, 32:64, :].astype(F32)
+        gl_o[0, k * 16:(k + 1) * 16, :] = fin[k, 64:80, :].astype(F32)
+    gate_grad(3)
+
     for n in range(4):
         wait_bytes(t1.at[pl.ds(0, INNER - 1)], a_send.at[n])
     wait_bytes(ls_r.at[pl.ds(0, XY - 1)], m_send.at[0])
@@ -401,17 +401,15 @@
         wait_bytes(half, l_sem.at[n])
         wait_bytes(half, e_send.at[n])
         wait_bytes(half, e_recv.at[n])
-    for out in outs:
-        out.wait()
-
-
-def body(inputs, gate_in, grad_out, right_factor, left_factor):
+
+
+def body(*operands):
     hbm = pl.BlockSpec(memory_space=pl.ANY)
     out_shape = (
-        jax.ShapeDtypeStruct((1, ROWS, Q, 2 * CG), BF16),
-        jax.ShapeDtypeStruct((1, ROWS, Q, 2 * CG), BF16),
-        jax.ShapeDtypeStruct((1, Q, Q), F32),
-        jax.ShapeDtypeStruct((1, P_ALL, P_ALL), F32),
+        pltpu.VMEM((1, ROWS, Q, 2 * CG), BF16),
+        pltpu.VMEM((1, ROWS, Q, 2 * CG), BF16),
+        pltpu.VMEM((1, Q, Q), F32),
+        pltpu.VMEM((1, P_ALL, P_ALL), F32),
     )
     blocks = pltpu.VMEM((INNER, BLK, CG), BF16)
     rows = pltpu.VMEM((CHIP, Q, CG), BF16)
@@ -422,8 +420,6 @@
         pltpu.VMEM((Q, Q), BF16),
         pltpu.VMEM((P_ALL, P_ALL), BF16),
         rows, rows,
-        pltpu.VMEM((Q, Q), F32),
-        pltpu.VMEM((P_ALL, P_ALL), F32),
         wide, wide, wide,
         columns, columns,
         rows,
@@ -448,13 +444,13 @@
         kernel,
         out_shape=out_shape,
         in_specs=[hbm] * 5,
-        out_specs=(hbm,) * 4,
+        out_specs=(pl.BlockSpec(memory_space=pltpu.VMEM),) * 4,
         scratch_shapes=scratch,
         compiler_params=pltpu.CompilerParams(
-            collective_id=0, has_side_effects=True, vmem_limit_bytes=48 * 1024 * 1024
+            collective_id=0, has_side_effects=True, vmem_limit_bytes=52 * 1024 * 1024
         ),
         cost_estimate=pl.CostEstimate(flops=4 * 10**9, bytes_accessed=12 * 10**6, transcendentals=3 * 10**6),
-    )(inputs, gate_in, grad_out, right_factor, left_factor)
+    )(*(pltpu.with_memory_space_constraint(a, pltpu.HBM) for a in operands))
 
 
 def solution(mesh):

time: 175 us -> 175 us (level)
  local copies, waits for them, and re-layouts: 6.13 us -> 3.96 us
  Pallas kernels: 168 us -> 170 us
    unnamed x8 -> x4, local copies, waits for them, and re-layouts: 6.13 us -> 3.96 us
where the time goes in v4:
time: 175 us
  Pallas kernels  170 us (97%)
  local copies, waits for them, and re-layouts  3.96 us (2%)
    pallas_call x1, Pallas kernels, body(): pl.pallas_call(kernel, out_shape=out_shape, in_specs=[hbm] * 5, out_specs...  170 us
    unnamed x4, local copies, waits for them, and re-layouts  3.96 us

profile of v4, /device:TPU:1, one launch (start us, length us, event | category | flops | bytes accessed | tf_op | source)
XLA Modules:
  0.0 174.7 jit_solution(15277887232780997595)
XLA Ops:
  0.6 170.1 %shard_map.84 = (bf16[1,2,512,768]{3,2,1,0:T(8,128)(2,1)S(1)}, bf16[1,2,512,768]{3,2,1,0:T(8,128)(2,1)S(1)}, f32[1,512,512]{2,1,0:T(8,128)S(1)}, f32[1,256,256]{2,1,0:T(8,128)S(1)}) custom-call(bf16[1,2,512,768]{3,2,1,0:T(8,128)(2,1)} %x_h.1, bf16[1,2,512,768]{3,2,1,0:T(8,128)(2,1)} %gate_h.1, bf16[1,2,512,768]{3,2,1,0:T(8,128)(2,1)} %gout_h.1, ...), custom_call_target="tpu_custom_call" | custom-call | flops 4000000000 | bytes 12000000 | tf_op jit(solution)/shard_map/pallas_call | solution.py:443
  170.7 1.1 copy.13
  171.9 0.7 copy.16
  172.6 1.0 copy.15
  173.5 1.1 copy.14

commit v5 on v4

--- a/solution.py
+++ b/solution.py
@@ -22,10 +22,10 @@
 BLK = CHIP * QB
 
 BEFORE_COLS = (0, 1)
-AFTER_COLS = (2,)
-AFTER_PLANE = (3,)
-AFTER_Z = (4, 5)
-AFTER_SHARES = (6, 7)
+AFTER_COLS = (2, 3)
+AFTER_PLANE = (4, 5)
+AFTER_Z = (6,)
+AFTER_SHARES = (7,)
 
 
 def gelu_value(mixed):
@@ -144,31 +144,48 @@
                 parts.append((a * b).reshape(4, QB, CG))
             s2[pl.ds(jj * 4, 4)] = jnp.concatenate(parts, axis=1).astype(BF16)
 
-    def send(src, dst, n, sem, e, first=0, last=ZH):
+    def send_to(src, dst, n, sem, ii):
+        pltpu.make_async_remote_copy(
+            src_ref=src.at[ii], dst_ref=dst.at[i], send_sem=a_send.at[n], recv_sem=a_recv.at[sem],
+            device_id={"inner": ii}, device_id_type=MESH,
+        ).start()
+
+    def send_chunk(src, dst, n, e, first=0, last=ZH):
+        each_partner(e, lambda ii: send_to(src, dst, n, 4 * n - 3 + e, ii), first, last)
+
+    def send_mixed(*pieces):
+        for k in pieces:
+            if k < 6:
+                send_chunk(t1, b1, 2, k // 2, k % 2 * 2, k % 2 * 2 + 2)
+            else:
+                for t in (k % 2 * 2, k % 2 * 2 + 1):
+                    def step(u, _):
+                        send_to(t1, b1, 2, 13 + t, place(3, t, 1) * ZH + lax.rem(zh + t + u, ZH))
+                        return 0
+
+                    lax.fori_loop(0, ZH, step, 0)
+
+    def wait_chunk(n, e):
+        wait_bytes(t1.at[pl.ds(0, 15 if e == 0 else 16)], a_recv.at[4 * n - 3 + e])
+
+    def send_half(h):
+        half = pl.ds(pl.multiple_of(h * 16, 16), 16)
+
         def act(ii):
             pltpu.make_async_remote_copy(
-                src_ref=src.at[ii], dst_ref=dst.at[i], send_sem=a_send.at[n], recv_sem=a_recv.at[sem],
+                src_ref=s1.at[ii, half], dst_ref=r1.at[i, half], send_sem=a_send.at[0], recv_sem=a_recv.at[0],
                 device_id={"inner": ii}, device_id_type=MESH,
             ).start()
 
-        each_partner(e, act, first, last)
-
-    def send_chunk(src, dst, n, e):
-        send(src, dst, n, 4 * n - 3 + e, e)
-
-    def send_mixed(*pieces):
-        for k in pieces:
-            send(t1, b1, 2, 5 + k // 2, k // 2, k % 2 * 2, k % 2 * 2 + 2)
-
-    def wait_chunk(n, e):
-        wait_bytes(t1.at[pl.ds(0, 15 if e == 0 else 16)], a_recv.at[4 * n - 3 + e])
-
+        for e in range(4):
+            each_partner(e, act)
+
+    send_half(c)
     gifts[0].wait_recv()
     gifts[1].start()
     gifts[2].start()
     right_mix(1 - c)
-    for e in range(4):
-        send(s1, r1, 0, 0, e)
+    send_half(1 - c)
     loads[1].wait()
     loads[2].wait()
     gifts[1].wait_recv()
@@ -272,17 +289,19 @@
             device_id={"outer": 1 - c}, device_id_type=MESH,
         ).start()
 
+    def gate_chip(jj):
+        rows = pl.ds(pl.multiple_of(jj * 32, 32), 32)
+        v = b1[pl.ds(jj * 4, 4)].astype(F32)
+        for p in range(CHIP):
+            act = gelu_value(v[:, p * QB:(p + 1) * QB, :].reshape(32, CG))
+            ggate_v[p, rows, :] = (gout[p, rows, :].astype(F32) * act).astype(BF16)
+        hand_out(ggate_v, ggate_o, rows, 6)
+
     def gate_grad(e):
         wait_chunk(2, e)
 
         def step(t, _):
-            jj = source(e, t)
-            rows = pl.ds(pl.multiple_of(jj * 32, 32), 32)
-            v = b1[pl.ds(jj * 4, 4)].astype(F32)
-            for p in range(CHIP):
-                act = gelu_value(v[:, p * QB:(p + 1) * QB, :].reshape(32, CG))
-                ggate_v[p, rows, :] = (gout[p, rows, :].astype(F32) * act).astype(BF16)
-            hand_out(ggate_v, ggate_o, rows, 6)
+            gate_chip(source(e, t))
             return 0
 
         lax.fori_loop(0, 4, step, 0)
@@ -388,7 +407,9 @@
         gr_o[0, k * 32:(k + 1) * 32, 0:256] = fin[k, 0:32, :].astype(F32)
         gr_o[0, k * 32:(k + 1) * 32, 256:512] = fin[k, 32:64, :].astype(F32)
         gl_o[0, k * 16:(k + 1) * 16, :] = fin[k, 64:80, :].astype(F32)
-    gate_grad(3)
+    for t in range(4):
+        wait_bytes(t1.at[pl.ds(0, ZH)], a_recv.at[13 + t])
+        gate_chip(place(3, t, -1))
 
     for n in range(4):
         wait_bytes(t1.at[pl.ds(0, INNER - 1)], a_send.at[n])
@@ -403,13 +424,27 @@
         wait_bytes(half, e_recv.at[n])
 
 
+def hand_on(*refs):
+    results, outputs, sem = refs[:4], refs[4:8], refs[8]
+    parts = []
+    for src, dst in zip(results[:2], outputs[:2]):
+        for p in range(ROWS):
+            parts.append((src.at[0, p], dst.at[0, p]))
+    parts.extend(zip(results[2:], outputs[2:]))
+    copies = [pltpu.make_async_copy(src, dst, sem.at[n]) for n, (src, dst) in enumerate(parts)]
+    for copy in copies:
+        copy.start()
+    for copy in copies:
+        copy.wait()
+
+
 def body(*operands):
     hbm = pl.BlockSpec(memory_space=pl.ANY)
-    out_shape = (
-        pltpu.VMEM((1, ROWS, Q, 2 * CG), BF16),
-        pltpu.VMEM((1, ROWS, Q, 2 * CG), BF16),
-        pltpu.VMEM((1, Q, Q), F32),
-        pltpu.VMEM((1, P_ALL, P_ALL), F32),
+    shapes = (
+        ((1, ROWS, Q, 2 * CG), BF16),
+        ((1, ROWS, Q, 2 * CG), BF16),
+        ((1, Q, Q), F32),
+        ((1, P_ALL, P_ALL), F32),
     )
     blocks = pltpu.VMEM((INNER, BLK, CG), BF16)
     rows = pltpu.VMEM((CHIP, Q, CG), BF16)
@@ -433,16 +468,16 @@
         pltpu.VMEM((8, 80, 256), BF16),
         pltpu.VMEM((XY, 80, 256), BF16),
         pltpu.SemaphoreType.DMA((4,)),
-        pltpu.SemaphoreType.DMA((13,)),
+        pltpu.SemaphoreType.DMA((17,)),
         pltpu.SemaphoreType.DMA((5,)),
         pltpu.SemaphoreType.DMA((5,)),
         pltpu.SemaphoreType.DMA((7,)),
         pltpu.SemaphoreType.DMA((7,)),
         pltpu.SemaphoreType.DMA((9,)),
     ]
-    return pl.pallas_call(
+    results = pl.pallas_call(
         kernel,
-        out_shape=out_shape,
+        out_shape=tuple(pltpu.VMEM(*shape) for shape in shapes),
         in_specs=[hbm] * 5,
         out_specs=(pl.BlockSpec(memory_space=pltpu.VMEM),) * 4,
         scratch_shapes=scratch,
@@ -451,6 +486,15 @@
         ),
         cost_estimate=pl.CostEstimate(flops=4 * 10**9, bytes_accessed=12 * 10**6, transcendentals=3 * 10**6),
     )(*(pltpu.with_memory_space_constraint(a, pltpu.HBM) for a in operands))
+    return pl.pallas_call(
+        hand_on,
+        out_shape=tuple(jax.ShapeDtypeStruct(*shape) for shape in shapes),
+        in_specs=[pl.BlockSpec(memory_space=pltpu.VMEM)] * 4,
+        out_specs=(hbm,) * 4,
+        scratch_shapes=[pltpu.SemaphoreType.DMA((6,))],
+        compiler_params=pltpu.CompilerParams(vmem_limit_bytes=8 * 1024 * 1024),
+        cost_estimate=pl.CostEstimate(flops=0, bytes_accessed=9 * 10**6, transcendentals=0),
+    )(*(pltpu.with_memory_space_constraint(a, pltpu.VMEM) for a in results))
 
 
 def solution(mesh):

time: 175 us -> 169 us (0.966)
  local copies, waits for them, and re-layouts: 3.96 us -> 0 us
  Pallas kernels: 170 us -> 168 us
    unnamed x4 -> x0, local copies, waits for them, and re-layouts: 3.96 us -> none
    pallas_call x1 -> x2, Pallas kernels: 170 us -> 168 us  [the longest x1 166 us: body(): pl.pallas_call(kernel, out_shape=tuple((pltpu.VMEM(*shape) for shape in s...]
where the time goes in v5:
time: 169 us
  Pallas kernels  168 us (99%)
    pallas_call x1, Pallas kernels, body(): pl.pallas_call(kernel, out_shape=tuple((pltpu.VMEM(*shape) for shape in s...  166 us

profile of v5, /device:TPU:1, one launch (start us, length us, event | category | flops | bytes accessed | tf_op | source)
XLA Modules:
  0.0 168.8 jit_solution(11283652655233121518)
XLA Ops:
  0.6 166.0 %shard_map.84 = (bf16[1,2,512,768]{3,2,1,0:T(8,128)(2,1)S(1)}, bf16[1,2,512,768]{3,2,1,0:T(8,128)(2,1)S(1)}, f32[1,512,512]{2,1,0:T(8,128)S(1)}, f32[1,256,256]{2,1,0:T(8,128)S(1)}) custom-call(bf16[1,2,512,768]{3,2,1,0:T(8,128)(2,1)} %x_h.1, bf16[1,2,512,768]{3,2,1,0:T(8,128)(2,1)} %gate_h.1, bf16[1,2,512,768]{3,2,1,0:T(8,128)(2,1)} %gout_h.1, ...), custom_call_target="tpu_custom_call" | custom-call | flops 4000000000 | bytes 12000000 | tf_op jit(solution)/shard_map/pallas_call | solution.py:478
  166.7 2.1 %shard_map.85 = (bf16[1,2,512,768]{3,2,1,0:T(8,128)(2,1)}, bf16[1,2,512,768]{3,2,1,0:T(8,128)(2,1)}, f32[1,512,512]{2,1,0:T(8,128)}, f32[1,256,256]{2,1,0:T(8,128)}) custom-call(bf16[1,2,512,768]{3,2,1,0:T(8,128)(2,1)S(1)} %get-tuple-element.8.refs_0_, bf16[1,2,512,768]{3,2,1,0:T(8,128)(2,1)S(1)} %get-tuple-element.9.refs_1_, ...), custom_call_target="tpu_custom_call" | custom-call | bytes 9000000 | tf_op jit(solution)/shard_map/pallas_call | solution.py:489

commit v6 on v5

--- a/solution.py
+++ b/solution.py
@@ -74,11 +74,6 @@
         return lax.rem(ys[0] + 8 - e - t, 4) * 4 + lax.rem(xs[0] + 4 - t, 4)
 
     def each_partner(e, act, first=0, last=ZH):
-        if e == 0 and first == 0:
-            for t in range(1, 4):
-                act(place(e, t, 1) * ZH + (zh + t) % ZH)
-            first = 1
-
         def step(u, _):
             for t in range(4):
                 act(place(e, t, 1) * ZH + lax.rem(zh + t + u, ZH))
@@ -99,15 +94,21 @@
     barrier = pltpu.get_barrier_semaphore()
 
     def greet(ii):
-        pl.semaphore_signal(barrier, inc=1, device_id={"inner": ii}, device_id_type=MESH)
+        pl.semaphore_signal(barrier, inc=1, device_id={"inner": ii, "dp": 1 - d}, device_id_type=MESH)
 
     pl.semaphore_signal(barrier, inc=1, device_id={"outer": 1 - c}, device_id_type=MESH)
     for e in range(4):
         each_partner(e, greet)
-    for k in range(ZH):
+    for k in range(1, ZH):
         pl.semaphore_signal(
-            barrier, inc=1, device_id={"inner": j * ZH + (zh + k) % ZH, "dp": 1 - d}, device_id_type=MESH
+            barrier, inc=1, device_id={"inner": j * ZH + (zh + k) % ZH}, device_id_type=MESH
         )
+
+    def greet_plane(k, _):
+        pl.semaphore_signal(barrier, inc=1, device_id={"inner": lax.rem(j + k, XY) * ZH + zh}, device_id_type=MESH)
+        return 0
+
+    lax.fori_loop(1, XY, greet_plane, 0)
 
     def right_mix(h):
         def step(m, _):
@@ -123,7 +124,7 @@
     loads[3].wait()
     right_mix(c)
 
-    pl.semaphore_wait(barrier, INNER + ZH)
+    pl.semaphore_wait(barrier, 1 + INNER + (ZH - 1) + (XY - 1))
     gifts = [
         pltpu.make_async_remote_copy(
             src_ref=src.at[0, :, :, theirs], dst_ref=dst.at[my_rows], send_sem=e_send.at[n], recv_sem=e_recv.at[n],
@@ -147,7 +148,7 @@
     def send_to(src, dst, n, sem, ii):
         pltpu.make_async_remote_copy(
             src_ref=src.at[ii], dst_ref=dst.at[i], send_sem=a_send.at[n], recv_sem=a_recv.at[sem],
-            device_id={"inner": ii}, device_id_type=MESH,
+            device_id={"inner": ii, "dp": 1 - d}, device_id_type=MESH,
         ).start()
 
     def send_chunk(src, dst, n, e, first=0, last=ZH):
@@ -166,7 +167,7 @@
                     lax.fori_loop(0, ZH, step, 0)
 
     def wait_chunk(n, e):
-        wait_bytes(t1.at[pl.ds(0, 15 if e == 0 else 16)], a_recv.at[4 * n - 3 + e])
+        wait_bytes(t1.at[pl.ds(0, XY)], a_recv.at[4 * n - 3 + e])
 
     def send_half(h):
         half = pl.ds(pl.multiple_of(h * 16, 16), 16)
@@ -174,7 +175,7 @@
         def act(ii):
             pltpu.make_async_remote_copy(
                 src_ref=s1.at[ii, half], dst_ref=r1.at[i, half], send_sem=a_send.at[0], recv_sem=a_recv.at[0],
-                device_id={"inner": ii}, device_id_type=MESH,
+                device_id={"inner": ii, "dp": 1 - d}, device_id_type=MESH,
             ).start()
 
         for e in range(4):
@@ -193,8 +194,6 @@
     for e in range(4):
         weigh(e)
         send_chunk(s2, r2, 1, e)
-    r1[i] = s1[i]
-    r2[i] = s2[i]
     loads[4].wait()
     lt[...] = lf[...].astype(F32).T.astype(BF16)
     for h in range(2):
@@ -203,7 +202,7 @@
     def column(q):
         return jnp.concatenate([wide_a[n, pl.ds(q, P_ALL, stride=QB), :] for n in range(LANES)], axis=1)
 
-    wait_bytes(t1.at[pl.ds(0, INNER - 1)], a_recv.at[0])
+    wait_bytes(t1, a_recv.at[0])
 
     def widen(m, _):
         v = r1[pl.ds(m * 4, 4)].reshape(128, CG).astype(F32)
@@ -226,7 +225,6 @@
         return 0
 
     lax.fori_loop(0, 32, narrow, 0)
-    b1[i] = t1[i]
     send_mixed(*BEFORE_COLS)
 
     def slopes(m, _):
@@ -262,7 +260,6 @@
                 v = wide_c[n, rows, :].astype(BF16)
                 t2[pl.ds(jj * 4, 4), :, n * 128:(n + 1) * 128] = v.reshape(4, BLK, 128)
         send_chunk(t2, b2, 3, e)
-    b2[i] = t2[i]
     send_mixed(*AFTER_COLS)
     gl_acc = jnp.zeros((P_ALL, P_ALL), F32)
     for q in range(QB):
@@ -412,7 +409,7 @@
         gate_chip(place(3, t, -1))
 
     for n in range(4):
-        wait_bytes(t1.at[pl.ds(0, INNER - 1)], a_send.at[n])
+        wait_bytes(t1, a_send.at[n])
     wait_bytes(ls_r.at[pl.ds(0, XY - 1)], m_send.at[0])
     wait_bytes(rs_r.at[pl.ds(0, XY - 1)], m_send.at[1])
     for gift in gifts:

time: 169 us -> 164 us (0.970)
  Pallas kernels: 168 us -> 164 us
    pallas_call x1, Pallas kernels: 166 us -> 161 us  [body(): pl.pallas_call(kernel, out_shape=tuple((pltpu.VMEM(*shape) for shape in s...]
where the time goes in v6:
time: 164 us
  Pallas kernels  164 us (100%)
    pallas_call x1, Pallas kernels, body(): pl.pallas_call(kernel, out_shape=tuple((pltpu.VMEM(*shape) for shape in s...  161 us

profile of v6, /device:TPU:1, one launch (start us, length us, event | category | flops | bytes accessed | tf_op | source)
XLA Modules:
  0.0 164.2 jit_solution(9763914516513290102)
XLA Ops:
  0.6 161.4 %shard_map.84 = (bf16[1,2,512,768]{3,2,1,0:T(8,128)(2,1)S(1)}, bf16[1,2,512,768]{3,2,1,0:T(8,128)(2,1)S(1)}, f32[1,512,512]{2,1,0:T(8,128)S(1)}, f32[1,256,256]{2,1,0:T(8,128)S(1)}) custom-call(bf16[1,2,512,768]{3,2,1,0:T(8,128)(2,1)} %x_h.1, bf16[1,2,512,768]{3,2,1,0:T(8,128)(2,1)} %gate_h.1, bf16[1,2,512,768]{3,2,1,0:T(8,128)(2,1)} %gout_h.1, ...), custom_call_target="tpu_custom_call" | custom-call | flops 4000000000 | bytes 12000000 | tf_op jit(solution)/shard_map/pallas_call | solution.py:475
  162.1 2.1 %shard_map.85 = (bf16[1,2,512,768]{3,2,1,0:T(8,128)(2,1)}, bf16[1,2,512,768]{3,2,1,0:T(8,128)(2,1)}, f32[1,512,512]{2,1,0:T(8,128)}, f32[1,256,256]{2,1,0:T(8,128)}) custom-call(bf16[1,2,512,768]{3,2,1,0:T(8,128)(2,1)S(1)} %get-tuple-element.8.refs_0_, bf16[1,2,512,768]{3,2,1,0:T(8,128)(2,1)S(1)} %get-tuple-element.9.refs_1_, ...), custom_call_target="tpu_custom_call" | custom-call | bytes 9000000 | tf_op jit(solution)/shard_map/pallas_call | solution.py:486

commit v7 on v6

--- a/solution.py
+++ b/solution.py
@@ -21,9 +21,9 @@
 QB = 8
 BLK = CHIP * QB
 
-BEFORE_COLS = (0, 1)
-AFTER_COLS = (2, 3)
-AFTER_PLANE = (4, 5)
+BEFORE_COLS = (0, 1, 2)
+AFTER_COLS = (3, 4)
+AFTER_PLANE = (5,)
 AFTER_Z = (6,)
 AFTER_SHARES = (7,)
 
@@ -73,10 +73,13 @@
     def source(e, t):
         return lax.rem(ys[0] + 8 - e - t, 4) * 4 + lax.rem(xs[0] + 4 - t, 4)
 
+    yc = [(j // 4 + n + 2 * c) % 4 for n in range(4)]
+    xc = [(j % 4 + n + 2 * c) % 4 for n in range(4)]
+
     def each_partner(e, act, first=0, last=ZH):
         def step(u, _):
             for t in range(4):
-                act(place(e, t, 1) * ZH + lax.rem(zh + t + u, ZH))
+                act((yc[(e + t) % 4] * 4 + xc[t]) * ZH + lax.rem(zh + t + u, ZH))
             return 0
 
         lax.fori_loop(first, last, step, 0)

time: 164 us -> 165 us (level)
  no operation moved by 1% of the time
where the time goes in v7:
time: 165 us
  Pallas kernels  164 us (99%)
    pallas_call x1, Pallas kernels, body(): pl.pallas_call(kernel, out_shape=tuple((pltpu.VMEM(*shape) for shape in s...  162 us

profile of v7, /device:TPU:1, one launch (start us, length us, event | category | flops | bytes accessed | tf_op | source)
XLA Modules:
  0.0 165.0 jit_solution(4951084615512218729)
XLA Ops:
  0.6 162.2 %shard_map.84 = (bf16[1,2,512,768]{3,2,1,0:T(8,128)(2,1)S(1)}, bf16[1,2,512,768]{3,2,1,0:T(8,128)(2,1)S(1)}, f32[1,512,512]{2,1,0:T(8,128)S(1)}, f32[1,256,256]{2,1,0:T(8,128)S(1)}) custom-call(bf16[1,2,512,768]{3,2,1,0:T(8,128)(2,1)} %x_h.1, bf16[1,2,512,768]{3,2,1,0:T(8,128)(2,1)} %gate_h.1, bf16[1,2,512,768]{3,2,1,0:T(8,128)(2,1)} %gout_h.1, ...), custom_call_target="tpu_custom_call" | custom-call | flops 4000000000 | bytes 12000000 | tf_op jit(solution)/shard_map/pallas_call | solution.py:478
  162.8 2.1 %shard_map.85 = (bf16[1,2,512,768]{3,2,1,0:T(8,128)(2,1)}, bf16[1,2,512,768]{3,2,1,0:T(8,128)(2,1)}, f32[1,512,512]{2,1,0:T(8,128)}, f32[1,256,256]{2,1,0:T(8,128)}) custom-call(bf16[1,2,512,768]{3,2,1,0:T(8,128)(2,1)S(1)} %get-tuple-element.8.refs_0_, bf16[1,2,512,768]{3,2,1,0:T(8,128)(2,1)S(1)} %get-tuple-element.9.refs_1_, ...), custom_call_target="tpu_custom_call" | custom-call | bytes 9000000 | tf_op jit(solution)/shard_map/pallas_call | solution.py:489

commit v8 on v7

--- a/solution.py
+++ b/solution.py
@@ -76,10 +76,15 @@
     yc = [(j // 4 + n + 2 * c) % 4 for n in range(4)]
     xc = [(j % 4 + n + 2 * c) % 4 for n in range(4)]
 
+    def along_z(n):
+        n = n % 4
+        dz = (1 - 2 * c) * (1 - 2 * (n % 2)) * (3 - 2 * (n // 2))
+        return (zh + d + (dz + 7) // 2) % ZH
+
     def each_partner(e, act, first=0, last=ZH):
         def step(u, _):
             for t in range(4):
-                act((yc[(e + t) % 4] * 4 + xc[t]) * ZH + lax.rem(zh + t + u, ZH))
+                act((yc[(e + t) % 4] * 4 + xc[t]) * ZH + along_z(t + u))
             return 0
 
         lax.fori_loop(first, last, step, 0)
@@ -164,7 +169,7 @@
             else:
                 for t in (k % 2 * 2, k % 2 * 2 + 1):
                     def step(u, _):
-                        send_to(t1, b1, 2, 13 + t, place(3, t, 1) * ZH + lax.rem(zh + t + u, ZH))
+                        send_to(t1, b1, 2, 13 + t, place(3, t, 1) * ZH + along_z(t + u))
                         return 0
 
                     lax.fori_loop(0, ZH, step, 0)
@@ -374,26 +379,46 @@
             total = total + zrecv[k].astype(F32)
         fin[j] = total.astype(BF16)
 
-        def give(k, _):
-            jj = (j + k) % XY
-            pltpu.make_async_remote_copy(
-                src_ref=fin.at[j], dst_ref=fin.at[j], send_sem=m_send.at[3], recv_sem=m_recv.at[3],
-                device_id={"inner": jj * ZH + zh}, device_id_type=MESH,
-            ).start()
-            return 0
-
-        lax.fori_loop(1, XY, give, 0)
+        for e in range(4):
+            for t in range(1 if e == 0 else 0, 4):
+                pltpu.make_async_remote_copy(
+                    src_ref=fin.at[j], dst_ref=fin.at[j], send_sem=m_send.at[3], recv_sem=m_recv.at[3 + e],
+                    device_id={"inner": place(e, t, 1) * ZH + zh}, device_id_type=MESH,
+                ).start()
 
     send_mixed(*AFTER_SHARES)
     gate_grad(2)
 
+    def last_gate(t):
+        wait_bytes(t1.at[pl.ds(0, ZH)], a_recv.at[13 + t])
+        gate_chip(place(3, t, -1))
+
+    def unpack():
+        for k in range(XY):
+            gr_o[0, k * 32:(k + 1) * 32, 0:256] = fin[k, 0:32, :].astype(F32)
+            gr_o[0, k * 32:(k + 1) * 32, 256:512] = fin[k, 32:64, :].astype(F32)
+            gl_o[0, k * 16:(k + 1) * 16, :] = fin[k, 64:80, :].astype(F32)
+
+    last_gate(0)
+    last_gate(1)
+
     @pl.when(d == c)
     def _():
-        wait_bytes(fin.at[pl.ds(0, XY - 1)], m_recv.at[3])
-        pltpu.make_async_remote_copy(
-            src_ref=fin, dst_ref=fin, send_sem=m_send.at[4], recv_sem=m_recv.at[4],
-            device_id={"outer": 1 - c}, device_id_type=MESH,
-        ).start()
+        for e in range(4):
+            wait_bytes(fin.at[pl.ds(0, 3 if e == 0 else 4)], m_recv.at[3 + e])
+            for t in range(4):
+                jj = place(e, t, -1)
+                pltpu.make_async_remote_copy(
+                    src_ref=fin.at[jj], dst_ref=fin.at[jj], send_sem=m_send.at[4], recv_sem=m_recv.at[7],
+                    device_id={"outer": 1 - c}, device_id_type=MESH,
+                ).start()
+        unpack()
+
+    last_gate(2)
+    last_gate(3)
+
+    @pl.when(d == c)
+    def _():
         wait_bytes(fin.at[pl.ds(0, XY - 1)], m_send.at[3])
         wait_bytes(zrecv.at[pl.ds(0, 3)], m_send.at[2])
         wait_bytes(fin, m_send.at[4])
@@ -401,15 +426,8 @@
     @pl.when(d != c)
     def _():
         wait_bytes(zrecv.at[pl.ds(0, 4)], m_send.at[2])
-        wait_bytes(fin, m_recv.at[4])
-
-    for k in range(XY):
-        gr_o[0, k * 32:(k + 1) * 32, 0:256] = fin[k, 0:32, :].astype(F32)
-        gr_o[0, k * 32:(k + 1) * 32, 256:512] = fin[k, 32:64, :].astype(F32)
-        gl_o[0, k * 16:(k + 1) * 16, :] = fin[k, 64:80, :].astype(F32)
-    for t in range(4):
-        wait_bytes(t1.at[pl.ds(0, ZH)], a_recv.at[13 + t])
-        gate_chip(place(3, t, -1))
+        wait_bytes(fin, m_recv.at[7])
+        unpack()
 
     for n in range(4):
         wait_bytes(t1, a_send.at[n])
@@ -470,7 +488,7 @@
         pltpu.SemaphoreType.DMA((4,)),
         pltpu.SemaphoreType.DMA((17,)),
         pltpu.SemaphoreType.DMA((5,)),
-        pltpu.SemaphoreType.DMA((5,)),
+        pltpu.SemaphoreType.DMA((8,)),
         pltpu.SemaphoreType.DMA((7,)),
         pltpu.SemaphoreType.DMA((7,)),
         pltpu.SemaphoreType.DMA((9,)),

time: 165 us -> 164 us (level)
  no operation moved by 1% of the time
where the time goes in v8:
time: 164 us
  Pallas kernels  163 us (99%)
    pallas_call x1, Pallas kernels, body(): pl.pallas_call(kernel, out_shape=tuple((pltpu.VMEM(*shape) for shape in s...  161 us

profile of v8, /device:TPU:1, one launch (start us, length us, event | category | flops | bytes accessed | tf_op | source)
XLA Modules:
  0.0 164.1 jit_solution(9451393485611127019)
XLA Ops:
  0.6 161.3 %shard_map.84 = (bf16[1,2,512,768]{3,2,1,0:T(8,128)(2,1)S(1)}, bf16[1,2,512,768]{3,2,1,0:T(8,128)(2,1)S(1)}, f32[1,512,512]{2,1,0:T(8,128)S(1)}, f32[1,256,256]{2,1,0:T(8,128)S(1)}) custom-call(bf16[1,2,512,768]{3,2,1,0:T(8,128)(2,1)} %x_h.1, bf16[1,2,512,768]{3,2,1,0:T(8,128)(2,1)} %gate_h.1, bf16[1,2,512,768]{3,2,1,0:T(8,128)(2,1)} %gout_h.1, ...), custom_call_target="tpu_custom_call" | custom-call | flops 4000000000 | bytes 12000000 | tf_op jit(solution)/shard_map/pallas_call | solution.py:496
  162.0 2.1 %shard_map.85 = (bf16[1,2,512,768]{3,2,1,0:T(8,128)(2,1)}, bf16[1,2,512,768]{3,2,1,0:T(8,128)(2,1)}, f32[1,512,512]{2,1,0:T(8,128)}, f32[1,256,256]{2,1,0:T(8,128)}) custom-call(bf16[1,2,512,768]{3,2,1,0:T(8,128)(2,1)S(1)} %get-tuple-element.8.refs_0_, bf16[1,2,512,768]{3,2,1,0:T(8,128)(2,1)S(1)} %get-tuple-element.9.refs_1_, ...), custom_call_target="tpu_custom_call" | custom-call | bytes 9000000 | tf_op jit(solution)/shard_map/pallas_call | solution.py:507

commit v9 on v8

--- a/solution.py
+++ b/solution.py
@@ -22,9 +22,9 @@
 BLK = CHIP * QB
 
 BEFORE_COLS = (0, 1, 2)
-AFTER_COLS = (3, 4)
-AFTER_PLANE = (5,)
-AFTER_Z = (6,)
+AMID_COLS = (3,)
+AFTER_PLANE = (4,)
+AFTER_Z = (5, 6)
 AFTER_SHARES = (7,)
 
 
@@ -52,7 +52,7 @@
     s1, s2, r1, r2, t1, t2, b1, b2,
     x, gate, gout, rf, lf, gin_v, ggate_v,
     wide_a, wide_b, wide_c, colsb, gmb, gcb, rt, lt,
-    rs_s, rs_r, ls_s, ls_r, share, zrecv, fin,
+    rs_s, rs_r, ls_s, ls_r, share, pair, zrecv, fin,
     a_send, a_recv, m_send, m_recv, e_send, e_recv, l_sem,
 ):
     i = lax.axis_index("inner")
@@ -268,7 +268,6 @@
                 v = wide_c[n, rows, :].astype(BF16)
                 t2[pl.ds(jj * 4, 4), :, n * 128:(n + 1) * 128] = v.reshape(4, BLK, 128)
         send_chunk(t2, b2, 3, e)
-    send_mixed(*AFTER_COLS)
     gl_acc = jnp.zeros((P_ALL, P_ALL), F32)
     for q in range(QB):
         gl_acc = gl_acc + dot(gmb[q], colsb[q], 1, 1)
@@ -331,6 +330,8 @@
         for t, jj in enumerate(spots):
             rs_s[jj] = total[t * 32:(t + 1) * 32, :].astype(BF16)
         scatter(rs_s, rs_r, 1, e)
+        if e == 1:
+            send_mixed(*AMID_COLS)
     rs_r[j] = rs_s[j]
     send_mixed(*AFTER_PLANE)
 
@@ -354,31 +355,34 @@
     share[32:64, :] = gr_sum[:, 256:512].astype(BF16)
     share[64:80, :] = gl_sum.astype(BF16)
 
-    def to_z(k):
-        return pltpu.make_async_remote_copy(
-            src_ref=share, dst_ref=zrecv.at[zh * 2 + d], send_sem=m_send.at[2], recv_sem=m_recv.at[2],
-            device_id={"inner": j * ZH + (zh + k) % ZH, "dp": c}, device_id_type=MESH,
-        )
-
-    for k in range(1, ZH):
-        to_z(k).start()
-
     @pl.when(d != c)
     def _():
-        to_z(0).start()
+        pltpu.make_async_remote_copy(
+            src_ref=share, dst_ref=pair, send_sem=m_send.at[2], recv_sem=m_recv.at[2],
+            device_id={"dp": c}, device_id_type=MESH,
+        ).start()
 
     send_mixed(*AFTER_Z)
-    gate_grad(1)
 
     @pl.when(d == c)
     def _():
-        zrecv[zh * 2 + d] = share[...]
-        wait_bytes(zrecv.at[pl.ds(0, 7)], m_recv.at[2])
+        wait_bytes(pair, m_recv.at[2])
+        zrecv[zh] = (share[...].astype(F32) + pair[...].astype(F32)).astype(BF16)
+        for k in range(1, ZH):
+            pltpu.make_async_remote_copy(
+                src_ref=zrecv.at[zh], dst_ref=zrecv.at[zh], send_sem=m_send.at[5], recv_sem=m_recv.at[8],
+                device_id={"inner": j * ZH + (zh + k) % ZH}, device_id_type=MESH,
+            ).start()
+
+    gate_grad(1)
+
+    @pl.when(d == c)
+    def _():
+        wait_bytes(zrecv.at[pl.ds(0, ZH - 1)], m_recv.at[8])
         total = zrecv[0].astype(F32)
-        for k in range(1, 8):
+        for k in range(1, ZH):
             total = total + zrecv[k].astype(F32)
         fin[j] = total.astype(BF16)
-
         for e in range(4):
             for t in range(1 if e == 0 else 0, 4):
                 pltpu.make_async_remote_copy(
@@ -420,12 +424,12 @@
     @pl.when(d == c)
     def _():
         wait_bytes(fin.at[pl.ds(0, XY - 1)], m_send.at[3])
-        wait_bytes(zrecv.at[pl.ds(0, 3)], m_send.at[2])
+        wait_bytes(zrecv.at[pl.ds(0, 3)], m_send.at[5])
         wait_bytes(fin, m_send.at[4])
 
     @pl.when(d != c)
     def _():
-        wait_bytes(zrecv.at[pl.ds(0, 4)], m_send.at[2])
+        wait_bytes(share, m_send.at[2])
         wait_bytes(fin, m_recv.at[7])
         unpack()
 
@@ -483,12 +487,13 @@
         pltpu.VMEM((XY, 16, P_ALL), BF16),
         pltpu.VMEM((XY, 16, P_ALL), BF16),
         pltpu.VMEM((80, 256), BF16),
-        pltpu.VMEM((8, 80, 256), BF16),
+        pltpu.VMEM((80, 256), BF16),
+        pltpu.VMEM((ZH, 80, 256), BF16),
         pltpu.VMEM((XY, 80, 256), BF16),
         pltpu.SemaphoreType.DMA((4,)),
         pltpu.SemaphoreType.DMA((17,)),
-        pltpu.SemaphoreType.DMA((5,)),
-        pltpu.SemaphoreType.DMA((8,)),
+        pltpu.SemaphoreType.DMA((6,)),
+        pltpu.SemaphoreType.DMA((9,)),
         pltpu.SemaphoreType.DMA((7,)),
         pltpu.SemaphoreType.DMA((7,)),
         pltpu.SemaphoreType.DMA((9,)),

time: 164 us -> 165 us (level)
  Pallas kernels: 163 us -> 165 us
where the time goes in v9:
time: 165 us
  Pallas kernels  165 us (100%)
    pallas_call x1, Pallas kernels, body(): pl.pallas_call(kernel, out_shape=tuple((pltpu.VMEM(*shape) for shape in s...  162 us

profile of v9, /device:TPU:1, one launch (start us, length us, event | category | flops | bytes accessed | tf_op | source)
XLA Modules:
  0.0 165.2 jit_solution(5210977747792737071)
XLA Ops:
  0.6 162.4 %shard_map.84 = (bf16[1,2,512,768]{3,2,1,0:T(8,128)(2,1)S(1)}, bf16[1,2,512,768]{3,2,1,0:T(8,128)(2,1)S(1)}, f32[1,512,512]{2,1,0:T(8,128)S(1)}, f32[1,256,256]{2,1,0:T(8,128)S(1)}) custom-call(bf16[1,2,512,768]{3,2,1,0:T(8,128)(2,1)} %x_h.1, bf16[1,2,512,768]{3,2,1,0:T(8,128)(2,1)} %gate_h.1, bf16[1,2,512,768]{3,2,1,0:T(8,128)(2,1)} %gout_h.1, ...), custom_call_target="tpu_custom_call" | custom-call | flops 4000000000 | bytes 12000000 | tf_op jit(solution)/shard_map/pallas_call | solution.py:501
  163.0 2.1 %shard_map.85 = (bf16[1,2,512,768]{3,2,1,0:T(8,128)(2,1)}, bf16[1,2,512,768]{3,2,1,0:T(8,128)(2,1)}, f32[1,512,512]{2,1,0:T(8,128)}, f32[1,256,256]{2,1,0:T(8,128)}) custom-call(bf16[1,2,512,768]{3,2,1,0:T(8,128)(2,1)S(1)} %get-tuple-element.8.refs_0_, bf16[1,2,512,768]{3,2,1,0:T(8,128)(2,1)S(1)} %get-tuple-element.9.refs_1_, ...), custom_call_target="tpu_custom_call" | custom-call | bytes 9000000 | tf_op jit(solution)/shard_map/pallas_call | solution.py:512

commit v10 on v9

--- a/solution.py
+++ b/solution.py
@@ -22,9 +22,10 @@
 BLK = CHIP * QB
 
 BEFORE_COLS = (0, 1, 2)
-AMID_COLS = (3,)
+AFTER_COLS = (3,)
 AFTER_PLANE = (4,)
-AFTER_Z = (5, 6)
+AFTER_PAIR = (5,)
+AFTER_Z = (6,)
 AFTER_SHARES = (7,)
 
 
@@ -268,6 +269,7 @@
                 v = wide_c[n, rows, :].astype(BF16)
                 t2[pl.ds(jj * 4, 4), :, n * 128:(n + 1) * 128] = v.reshape(4, BLK, 128)
         send_chunk(t2, b2, 3, e)
+    send_mixed(*AFTER_COLS)
     gl_acc = jnp.zeros((P_ALL, P_ALL), F32)
     for q in range(QB):
         gl_acc = gl_acc + dot(gmb[q], colsb[q], 1, 1)
@@ -330,8 +332,6 @@
         for t, jj in enumerate(spots):
             rs_s[jj] = total[t * 32:(t + 1) * 32, :].astype(BF16)
         scatter(rs_s, rs_r, 1, e)
-        if e == 1:
-            send_mixed(*AMID_COLS)
     rs_r[j] = rs_s[j]
     send_mixed(*AFTER_PLANE)
 
@@ -362,7 +362,7 @@
             device_id={"dp": c}, device_id_type=MESH,
         ).start()
 
-    send_mixed(*AFTER_Z)
+    send_mixed(*AFTER_PAIR)
 
     @pl.when(d == c)
     def _():
@@ -374,6 +374,7 @@
                 device_id={"inner": j * ZH + (zh + k) % ZH}, device_id_type=MESH,
             ).start()
 
+    send_mixed(*AFTER_Z)
     gate_grad(1)
 
     @pl.when(d == c)

time: 165 us -> 165 us (level)
  no operation moved by 1% of the time
where the time goes in v10:
time: 165 us
  Pallas kernels  164 us (99%)
    pallas_call x1, Pallas kernels, body(): pl.pallas_call(kernel, out_shape=tuple((pltpu.VMEM(*shape) for shape in s...  162 us

profile of v10, /device:TPU:1, one launch (start us, length us, event | category | flops | bytes accessed | tf_op | source)
XLA Modules:
  0.0 164.6 jit_solution(15414359680084922466)
XLA Ops:
  0.6 161.8 %shard_map.84 = (bf16[1,2,512,768]{3,2,1,0:T(8,128)(2,1)S(1)}, bf16[1,2,512,768]{3,2,1,0:T(8,128)(2,1)S(1)}, f32[1,512,512]{2,1,0:T(8,128)S(1)}, f32[1,256,256]{2,1,0:T(8,128)S(1)}) custom-call(bf16[1,2,512,768]{3,2,1,0:T(8,128)(2,1)} %x_h.1, bf16[1,2,512,768]{3,2,1,0:T(8,128)(2,1)} %gate_h.1, bf16[1,2,512,768]{3,2,1,0:T(8,128)(2,1)} %gout_h.1, ...), custom_call_target="tpu_custom_call" | custom-call | flops 4000000000 | bytes 12000000 | tf_op jit(solution)/shard_map/pallas_call | solution.py:502
  162.4 2.1 %shard_map.85 = (bf16[1,2,512,768]{3,2,1,0:T(8,128)(2,1)}, bf16[1,2,512,768]{3,2,1,0:T(8,128)(2,1)}, f32[1,512,512]{2,1,0:T(8,128)}, f32[1,256,256]{2,1,0:T(8,128)}) custom-call(bf16[1,2,512,768]{3,2,1,0:T(8,128)(2,1)S(1)} %get-tuple-element.8.refs_0_, bf16[1,2,512,768]{3,2,1,0:T(8,128)(2,1)S(1)} %get-tuple-element.9.refs_1_, ...), custom_call_target="tpu_custom_call" | custom-call | bytes 9000000 | tf_op jit(solution)/shard_map/pallas_call | solution.py:513

commit v11 on v8

--- a/solution.py
+++ b/solution.py
@@ -21,9 +21,9 @@
 QB = 8
 BLK = CHIP * QB
 
-BEFORE_COLS = (0, 1, 2)
-AFTER_COLS = (3, 4)
-AFTER_PLANE = (5,)
+BEFORE_COLS = (0, 1)
+AFTER_COLS = (2, 3)
+AFTER_PLANE = (4, 5)
 AFTER_Z = (6,)
 AFTER_SHARES = (7,)
 

time: 164 us -> 163 us (level)
  no operation moved by 1% of the time
where the time goes in v11:
time: 163 us
  Pallas kernels  163 us (100%)
    pallas_call x1, Pallas kernels, body(): pl.pallas_call(kernel, out_shape=tuple((pltpu.VMEM(*shape) for shape in s...  160 us

profile of v11, /device:TPU:1, one launch (start us, length us, event | category | flops | bytes accessed | tf_op | source)
XLA Modules:
  0.0 163.2 jit_solution(15021013916752727344)
XLA Ops:
  0.6 160.4 %shard_map.84 = (bf16[1,2,512,768]{3,2,1,0:T(8,128)(2,1)S(1)}, bf16[1,2,512,768]{3,2,1,0:T(8,128)(2,1)S(1)}, f32[1,512,512]{2,1,0:T(8,128)S(1)}, f32[1,256,256]{2,1,0:T(8,128)S(1)}) custom-call(bf16[1,2,512,768]{3,2,1,0:T(8,128)(2,1)} %x_h.1, bf16[1,2,512,768]{3,2,1,0:T(8,128)(2,1)} %gate_h.1, bf16[1,2,512,768]{3,2,1,0:T(8,128)(2,1)} %gout_h.1, ...), custom_call_target="tpu_custom_call" | custom-call | flops 4000000000 | bytes 12000000 | tf_op jit(solution)/shard_map/pallas_call | solution.py:496
  161.1 2.1 %shard_map.85 = (bf16[1,2,512,768]{3,2,1,0:T(8,128)(2,1)}, bf16[1,2,512,768]{3,2,1,0:T(8,128)(2,1)}, f32[1,512,512]{2,1,0:T(8,128)}, f32[1,256,256]{2,1,0:T(8,128)}) custom-call(bf16[1,2,512,768]{3,2,1,0:T(8,128)(2,1)S(1)} %get-tuple-element.8.refs_0_, bf16[1,2,512,768]{3,2,1,0:T(8,128)(2,1)S(1)} %get-tuple-element.9.refs_1_, ...), custom_call_target="tpu_custom_call" | custom-call | bytes 9000000 | tf_op jit(solution)/shard_map/pallas_call | solution.py:507

commit v12 on v11

--- a/solution.py
+++ b/solution.py
@@ -21,11 +21,11 @@
 QB = 8
 BLK = CHIP * QB
 
-BEFORE_COLS = (0, 1)
-AFTER_COLS = (2, 3)
-AFTER_PLANE = (4, 5)
-AFTER_Z = (6,)
-AFTER_SHARES = (7,)
+BEFORE_COLS = (0,)
+AFTER_COLS = (1, 2)
+AFTER_PLANE = (3, 4)
+AFTER_Z = (5,)
+AFTER_SHARES = (6, 7)
 
 
 def gelu_value(mixed):
@@ -311,8 +311,6 @@
 
         lax.fori_loop(0, 4, step, 0)
 
-    gate_grad(0)
-
     for e in range(4):
         wait_chunk(3, e)
         spots = [place(e, t, -1) for t in range(4)]
@@ -343,6 +341,8 @@
 
     lax.fori_loop(0, 4, input_grad, 0)
 
+    gate_grad(0)
+
     wait_bytes(ls_r.at[pl.ds(0, XY - 1)], m_recv.at[0])
     wait_bytes(rs_r.at[pl.ds(0, XY - 1)], m_recv.at[1])
     gr_sum = rs_r[0].astype(F32)
@@ -398,9 +398,6 @@
             gr_o[0, k * 32:(k + 1) * 32, 0:256] = fin[k, 0:32, :].astype(F32)
             gr_o[0, k * 32:(k + 1) * 32, 256:512] = fin[k, 32:64, :].astype(F32)
             gl_o[0, k * 16:(k + 1) * 16, :] = fin[k, 64:80, :].astype(F32)
-
-    last_gate(0)
-    last_gate(1)
 
     @pl.when(d == c)
     def _():
@@ -414,8 +411,8 @@
                 ).start()
         unpack()
 
-    last_gate(2)
-    last_gate(3)
+    for t in range(4):
+        last_gate(t)
 
     @pl.when(d == c)
     def _():

time: 163 us -> 163 us (level)
  no operation moved by 1% of the time
where the time goes in v12:
time: 163 us
  Pallas kernels  162 us (99%)
    pallas_call x1, Pallas kernels, body(): pl.pallas_call(kernel, out_shape=tuple((pltpu.VMEM(*shape) for shape in s...  160 us

profile of v12, /device:TPU:1, one launch (start us, length us, event | category | flops | bytes accessed | tf_op | source)
XLA Modules:
  0.0 163.1 jit_solution(9242949170327585479)
XLA Ops:
  0.6 160.3 %shard_map.84 = (bf16[1,2,512,768]{3,2,1,0:T(8,128)(2,1)S(1)}, bf16[1,2,512,768]{3,2,1,0:T(8,128)(2,1)S(1)}, f32[1,512,512]{2,1,0:T(8,128)S(1)}, f32[1,256,256]{2,1,0:T(8,128)S(1)}) custom-call(bf16[1,2,512,768]{3,2,1,0:T(8,128)(2,1)} %x_h.1, bf16[1,2,512,768]{3,2,1,0:T(8,128)(2,1)} %gate_h.1, bf16[1,2,512,768]{3,2,1,0:T(8,128)(2,1)} %gout_h.1, ...), custom_call_target="tpu_custom_call" | custom-call | flops 4000000000 | bytes 12000000 | tf_op jit(solution)/shard_map/pallas_call | solution.py:493
  160.9 2.1 %shard_map.85 = (bf16[1,2,512,768]{3,2,1,0:T(8,128)(2,1)}, bf16[1,2,512,768]{3,2,1,0:T(8,128)(2,1)}, f32[1,512,512]{2,1,0:T(8,128)}, f32[1,256,256]{2,1,0:T(8,128)}) custom-call(bf16[1,2,512,768]{3,2,1,0:T(8,128)(2,1)S(1)} %get-tuple-element.8.refs_0_, bf16[1,2,512,768]{3,2,1,0:T(8,128)(2,1)S(1)} %get-tuple-element.9.refs_1_, ...), custom_call_target="tpu_custom_call" | custom-call | bytes 9000000 | tf_op jit(solution)/shard_map/pallas_call | solution.py:504
